TPU v7x, 32 devices: a whole 2x2x4 slice. The times are simulated.
32 devices in a mesh: groups: 2 (over y), lon: 4 (over z), lat: 2 (over x), tm: 2 (over core).
Axes of the slice: x: 2, y: 2, z: 4, core: 2. Of those that a mesh axis runs over, the one named last changes fastest.
Arguments:
- kappa_squared: float32 [512, 1024], P('lat', 'lon'), may hold values from 0.05 to 1
- time_coupling: float32 [512, 1024], P('lat', 'lon'), may hold values from 0.3 to 0.95
- station_value: float32 [16384], P(('groups', 'lon', 'lat', 'tm')), parts along dimension 0, may hold values from -8 to 8
- station_weight: float32 [16384], P(('groups', 'lon', 'lat', 'tm')), parts along dimension 0, may hold values from 0.5 to 4
- station_cell: int32 [3, 16384], P(None, ('groups', 'lon', 'lat', 'tm')), parts along dimension 1, may hold values from 0 to 1023, as said below
- slab_blocks: int32 [8], P(('groups', 'lon')), parts along dimension 0, may hold values from 1 to 4, as said below
Outputs:
- kriged_field: float32 [16, 512, 1024], P(('groups', 'tm'), 'lat', 'lon'), parts along dimension 0
- station_fit: float32 [16384], P(('groups', 'lon', 'lat', 'tm')), parts along dimension 0
There are 2 independent parts, one for each index of `groups`. A program takes and returns all parts, laid end to end along the dimension named above; an argument that names none is the same for every part. Nothing has to cross between parts.
Inputs may be any that keep to these rules, and one draw needn't show every extreme that they name: `station_cell`: rows are longitude, latitude, hour. A row held by a device of longitude slab s has longitude in s * 256 to (s + 1) * 256 - 1. Among each device's 512 rows, padding included, every pair of a latitude band of 256 latitudes and an hour group of 4 hours is named by exactly 128 rows. The longitude 1024 - 1 is named in every draw. Every device of slab s holds its live stations in its first 128 * slab_blocks[s] rows. Some slab is full.
All inputs are finite; a program needn't handle non-finite values.
Results may differ from a plain program's by a relative error of at most 0.0001.
Values sent between devices are 32-bit elements; how exact they have to be, the bound alone decides.
A program may use at most 64 MiB of HBM per device.

v0:
```python
import jax
import jax.numpy as jnp
from jax import lax
from jax.sharding import PartitionSpec as P

HOURS = 8
ITERS = 2
BLOCK = 128


def extended_2(block, sides, width, periodic):
    for axis, dim in sides:
        count = lax.axis_size(axis)
        forward = [(i, i + 1) for i in range(count - 1)]
        if periodic:
            forward.append((count - 1, 0))
        backward = [(target, source) for source, target in forward]
        low = lax.ppermute(
            lax.slice_in_dim(block, block.shape[dim] - width, None, axis=dim), axis, forward
        )
        high = lax.ppermute(lax.slice_in_dim(block, 0, width, axis=dim), axis, backward)
        block = jnp.concatenate([low, block, high], axis=dim)
    return block


def outside_mask(count, width, at_first, at_last):
    position = jnp.arange(count + 2 * width)
    outside = (position < width) & at_first | (position >= count + width) & at_last
    return jnp.where(outside, 0.0, 1.0).astype(jnp.float32)


def lat_keep(count, width):
    return outside_mask(
        count, width, lax.axis_index("lat") == 0, lax.axis_index("lat") == lax.axis_size("lat") - 1
    )


def stiffen(extended, kappa_squared):
    centre = extended[..., 1:-1, 1:-1]
    beside_all = (
        extended[..., 1:-1, 2:]
        + extended[..., 1:-1, :-2]
        + extended[..., 2:, 1:-1]
        + extended[..., :-2, 1:-1]
    )
    return (kappa_squared + 1.0) * centre - 0.25 * beside_all


def couple(below, middle, above, time_coupling, hours_first):
    hour_index = hours_first + jnp.arange(middle.shape[0])
    at_edge = (hour_index == 0) | (hour_index == HOURS - 1)
    diagonal = jnp.where(
        at_edge[:, None, None], jnp.ones_like(time_coupling), 1.0 + time_coupling * time_coupling
    )
    return diagonal * middle - time_coupling * (below + above)


def body(kappa_squared, time_coupling, station_value, station_weight, station_cell, slab_blocks):
    lat_rows, lon_cols = kappa_squared.shape
    hours_dev = HOURS // lax.axis_size("tm")
    hours_first = lax.axis_index("tm") * hours_dev
    grid_shape = (hours_dev, lat_rows, lon_cols)
    row_count = station_value.shape[0]
    owners = lax.axis_size("lat") * lax.axis_size("tm")
    capacity = row_count // owners
    is_live = jnp.arange(row_count) < slab_blocks[0] * BLOCK
    owner_index = station_cell[1] // lat_rows * lax.axis_size("tm") + station_cell[2] // hours_dev
    one_hot = (owner_index[:, None] == jnp.arange(owners)[None, :]).astype(jnp.int32)
    rank_within = jnp.sum((jnp.cumsum(one_hot, axis=0) - 1) * one_hot, axis=1)
    slot_index = owner_index * capacity + rank_within
    target = jnp.where(is_live, slot_index, row_count)
    local_cell = (
        station_cell[2] % hours_dev * lat_rows + station_cell[1] % lat_rows
    ) * lon_cols + station_cell[0] % lon_cols
    payload = (
        jnp.zeros((2, row_count), jnp.float32)
        .at[:, target]
        .set(jnp.stack([station_value, station_weight]), mode="drop")
    )
    cell_slots = (
        jnp.zeros((1, row_count), jnp.int32).at[:, target].set(local_cell[None, :], mode="drop")
    )
    arrived, arrived_cells = (
        lax.all_to_all(payload, ("lat", "tm"), split_axis=1, concat_axis=1, tiled=True),
        lax.all_to_all(cell_slots, ("lat", "tm"), split_axis=1, concat_axis=1, tiled=True),
    )
    cells_here = arrived_cells[0]
    cell_total = hours_dev * lat_rows * lon_cols
    observed = jnp.zeros(cell_total, jnp.float32).at[cells_here].add(arrived[1]).reshape(grid_shape)
    right_side = (
        jnp.zeros(cell_total, jnp.float32)
        .at[cells_here]
        .add(arrived[1] * arrived[0])
        .reshape(grid_shape)
    )
    near_lat = lat_keep(lat_rows, 1)[None, :, None]

    def stiff_pass(values_in):
        extended = extended_2(values_in, (("lon", 2), ("lat", 1)), 1, True)
        return stiffen(extended * near_lat, kappa_squared)

    def square_sum(vector):
        return lax.psum(jnp.sum(vector * vector), ("lon", "lat", "tm"))

    solution = jnp.zeros(grid_shape, jnp.float32)
    residual = right_side
    direction = right_side
    norm_now = square_sum(residual)
    for iteration in range(ITERS):
        stiffened = stiff_pass(direction)
        layered = extended_2(stiffened, (("tm", 0),), 1, False)
        coupled = couple(layered[:-2], layered[1:-1], layered[2:], time_coupling, hours_first)
        applied = stiff_pass(coupled) + observed * direction
        step_length = norm_now / lax.psum(jnp.sum(direction * applied), ("lon", "lat", "tm"))
        solution = solution + step_length * direction
        if iteration + 1 < ITERS:
            residual = residual - step_length * applied
            norm_next = square_sum(residual)
            direction = residual + norm_next / norm_now * direction
            norm_now = norm_next
    picked = solution.reshape(-1)[cells_here][None, :]
    returned = lax.all_to_all(picked, ("lat", "tm"), split_axis=1, concat_axis=1, tiled=True)
    fitted = returned[0][slot_index]
    station_fit = jnp.where(is_live, fitted, jnp.zeros_like(fitted))
    return (solution, station_fit)


def solution(mesh):
    placed = (
        P("lat", "lon"),
        P("lat", "lon"),
        P(("groups", "lon", "lat", "tm")),
        P(("groups", "lon", "lat", "tm")),
        P(None, ("groups", "lon", "lat", "tm")),
        P(("groups", "lon")),
    )
    return jax.shard_map(
        body,
        mesh=mesh,
        in_specs=placed,
        out_specs=(P(("groups", "tm"), "lat", "lon"), P(("groups", "lon", "lat", "tm"))),
        check_vma=False,
    )
```

profile of v0, /device:TPU:0, one launch (start us, length us, event | category | flops | bytes accessed | tf_op | source)
XLA Modules:
  0.0 287.8 jit_solution(13460279823113159942)
XLA Ops:
  4.7 3.0 %scatter_custom_fusion = s32[512]{0:T(512)} fusion(s32[512]{0:T(512)S(1)} %bitcast.78, s32[512]{0:T(512)S(1)} %bitcast.82, s32[]{:T(128)} %constant.79.clone.1), kind=kCustom, calls=%fused_computation.158 | custom fusion | bytes 2052 | tf_op jit(solution)/shard_map/scatter | solution.py:81
  7.7 4.2 %all-to-all-start = ((s32[1,4,128]{2,0,1:T(1,128)}), s32[1,4,128]{2,0,1:T(1,128)S(1)}, u32[]{:S(2)}, u32[]{:S(2)}) async-start(s32[1,4,128]{2,0,1:T(1,128)} %bitcast.11), calls=%async_computation | async-start | bytes 4096 | tf_op jit(solution)/shard_map/all_to_all | solution.py:85
  15.6 3.2 %all-to-all-start.1 = ((f32[2,4,128]{2,0,1:T(2,128)}), f32[2,4,128]{2,0,1:T(2,128)S(1)}, u32[]{:S(2)}, u32[]{:S(2)}) async-start(f32[2,4,128]{2,0,1:T(2,128)} %copy.11), calls=%async_computation.1 | async-start | bytes 8192 | tf_op jit(solution)/shard_map/all_to_all | solution.py:84
  18.9 3.7 %all-to-all-done.1 = f32[2,4,128]{2,0,1:T(2,128)S(1)} async-done(((f32[2,4,128]{2,0,1:T(2,128)}), f32[2,4,128]{2,0,1:T(2,128)S(1)}, u32[]{:S(2)}, u32[]{:S(2)}) %all-to-all-start.1) | async-done | bytes 4128 | tf_op jit(solution)/shard_map/all_to_all | solution.py:84
  22.6 3.5 %scatter_custom_fusion.2 = f32[262144]{0:T(1024)S(1)} fusion(s32[512]{0:T(512)S(1)} %bitcast.70, f32[512]{0:T(512)S(1)} %mul.211, f32[]{:T(128)} %constant.78.clone.1), kind=kCustom, calls=%fused_computation.58 | custom fusion | flops 512 | bytes 1048580 | tf_op jit(solution)/shard_map/scatter-add | solution.py:93
  27.6 2.0 collective-permute-start
  29.6 2.0 collective-permute-start.1
  31.7 13.0 %collective-permute-done = f32[4,256,1]{2,1,0:T(8,128)S(1)} collective-permute-done((f32[4,256,1]{2,1,0:T(8,128)}, f32[4,256,1]{2,1,0:T(8,128)S(1)}, u32[]{:S(2)}, u32[]{:S(2)}) %collective-permute-start) | collective-permute-done | bytes 4128 | tf_op jit(solution)/shard_map/ppermute | solution.py:18
  44.6 10.0 %collective-permute-done.1 = f32[4,256,1]{2,1,0:T(8,128)S(1)} collective-permute-done((f32[4,256,1]{2,1,0:T(8,128)}, f32[4,256,1]{2,1,0:T(8,128)S(1)}, u32[]{:S(2)}, u32[]{:S(2)}) %collective-permute-start.1) | collective-permute-done | bytes 4128 | tf_op jit(solution)/shard_map/ppermute | solution.py:21
  54.9 1.9 collective-permute-start.3
  63.1 2.1 collective-permute-done.5
  66.6 2.9 %collective-permute-start.7 = (f32[4,256,1]{2,1,0:T(8,128)S(1)}, f32[4,256,1]{2,1,0:T(8,128)S(1)}, u32[]{:S(2)}, u32[]{:S(2)}) collective-permute-start(f32[4,256,1]{2,1,0:T(8,128)S(1)} %get-tuple-element.23), channel_id=1, source_target_pairs={{4,0},{8,4},{12,8},{0,12},{5,1},{9,5},{13,9},{1,13},{6,2},{10,6},{... | collective-permute-start | bytes 12296 | tf_op jit(solution)/shard_map/ppermute | solution.py:21
  69.6 12.8 %collective-permute-done.6 = f32[4,256,1]{2,1,0:T(8,128)S(1)} collective-permute-done((f32[4,256,1]{2,1,0:T(8,128)S(1)}, f32[4,256,1]{2,1,0:T(8,128)S(1)}, u32[]{:S(2)}, u32[]{:S(2)}) %collective-permute-start.6) | collective-permute-done | bytes 4128 | tf_op jit(solution)/shard_map/ppermute | solution.py:18
  82.4 9.2 %collective-permute-done.7 = f32[4,256,1]{2,1,0:T(8,128)S(1)} collective-permute-done((f32[4,256,1]{2,1,0:T(8,128)S(1)}, f32[4,256,1]{2,1,0:T(8,128)S(1)}, u32[]{:S(2)}, u32[]{:S(2)}) %collective-permute-start.7) | collective-permute-done | bytes 4128 | tf_op jit(solution)/shard_map/ppermute | solution.py:21
  95.3 3.7 %scatter_custom_fusion.3 = f32[262144]{0:T(1024)S(1)} fusion(s32[512]{0:T(512)S(1)} %bitcast.71, f32[512]{0:T(512)S(1)} %bitcast.75, f32[]{:T(128)} %constant.78.clone.1), kind=kCustom, calls=%fused_computation.56 | custom fusion | flops 512 | bytes 1048580 | tf_op jit(solution)/shard_map/scatter-add | solution.py:89
  100.3 2.0 maximum_multiply_fusion.1
  104.1 31.9 %all-reduce = (f32[]{:T(128)}, f32[]{:T(128)}) all-reduce(f32[]{:T(128)} %multiply_reduce_fusion.2, f32[]{:T(128)} %get-tuple-element.6), channel_id=1, replica_groups=mesh['groups'=2,'lon'=4,'lat'=2,'tm'=2] {'lon','lat','tm'}, use_global_device_ids=true, to_apply=%region_7.8 | all-reduce | flops 2 | bytes 16 | tf_op jit(solution)/shard_map/psum | solution.py:103
  138.1 30.1 %psum.30 = f32[]{:T(128)} all-reduce(f32[]{:T(128)} %multiply_reduce_fusion), channel_id=1, replica_groups=mesh['groups'=2,'lon'=4,'lat'=2,'tm'=2] {'lon','lat','tm'}, use_global_device_ids=true, to_apply=%region_12.13 | all-reduce | flops 1 | bytes 8 | tf_op jit(solution)/shard_map/psum | solution.py:103
  170.0 3.8 %collective-permute-start.11 = (f32[4,256,1]{2,1,0:T(8,128)S(1)}, f32[4,256,1]{2,1,0:T(8,128)S(1)}, u32[]{:S(2)}, u32[]{:S(2)}) collective-permute-start(f32[4,256,1]{2,1,0:T(8,128)S(1)} %get-tuple-element.21), channel_id=1, source_target_pairs={{4,0},{8,4},{12,8},{0,12},{5,1},{9,5},{13,9},{1,13},{6,2},{10,6},{... | collective-permute-start | bytes 12296 | tf_op jit(solution)/shard_map/ppermute | solution.py:21
  173.8 12.8 %collective-permute-done.10 = f32[4,256,1]{2,1,0:T(8,128)S(1)} collective-permute-done((f32[4,256,1]{2,1,0:T(8,128)S(1)}, f32[4,256,1]{2,1,0:T(8,128)S(1)}, u32[]{:S(2)}, u32[]{:S(2)}) %collective-permute-start.10) | collective-permute-done | bytes 4128 | tf_op jit(solution)/shard_map/ppermute | solution.py:18
  186.6 8.4 %collective-permute-done.11 = f32[4,256,1]{2,1,0:T(8,128)S(1)} collective-permute-done((f32[4,256,1]{2,1,0:T(8,128)S(1)}, f32[4,256,1]{2,1,0:T(8,128)S(1)}, u32[]{:S(2)}, u32[]{:S(2)}) %collective-permute-start.11) | collective-permute-done | bytes 4128 | tf_op jit(solution)/shard_map/ppermute | solution.py:21
  195.1 2.0 collective-permute-start.13
  203.4 2.1 collective-permute-done.15
  206.0 3.8 %collective-permute-start.17 = (f32[4,256,1]{2,1,0:T(8,128)S(1)}, f32[4,256,1]{2,1,0:T(8,128)S(1)}, u32[]{:S(2)}, u32[]{:S(2)}) collective-permute-start(f32[4,256,1]{2,1,0:T(8,128)S(1)} %get-tuple-element.17), channel_id=1, source_target_pairs={{4,0},{8,4},{12,8},{0,12},{5,1},{9,5},{13,9},{1,13},{6,2},{10,6},{... | collective-permute-start | bytes 12296 | tf_op jit(solution)/shard_map/ppermute | solution.py:21
  209.9 12.8 %collective-permute-done.16 = f32[4,256,1]{2,1,0:T(8,128)S(1)} collective-permute-done((f32[4,256,1]{2,1,0:T(8,128)S(1)}, f32[4,256,1]{2,1,0:T(8,128)S(1)}, u32[]{:S(2)}, u32[]{:S(2)}) %collective-permute-start.16) | collective-permute-done | bytes 4128 | tf_op jit(solution)/shard_map/ppermute | solution.py:18
  222.6 9.5 %collective-permute-done.17 = f32[4,256,1]{2,1,0:T(8,128)S(1)} collective-permute-done((f32[4,256,1]{2,1,0:T(8,128)S(1)}, f32[4,256,1]{2,1,0:T(8,128)S(1)}, u32[]{:S(2)}, u32[]{:S(2)}) %collective-permute-start.17) | collective-permute-done | bytes 4128 | tf_op jit(solution)/shard_map/ppermute | solution.py:21
  232.2 2.0 collective-permute-start.18
  240.4 30.1 %psum.31 = f32[]{:T(128)} all-reduce(f32[]{:T(128)} %fusion.6), channel_id=1, replica_groups=mesh['groups'=2,'lon'=4,'lat'=2,'tm'=2] {'lon','lat','tm'}, use_global_device_ids=true, to_apply=%region_14.15 | all-reduce | flops 1 | bytes 8 | tf_op jit(solution)/shard_map/psum | solution.py:114
  272.6 4.3 %gather_fusion = f32[512]{0:T(512)} fusion(f32[262144]{0:T(1024)S(1)} %bitcast.62, s32[1024]{0:T(1024)S(1)} %pad_clamp_fusion.1), kind=kCustom, calls=%fused_computation | custom fusion | bytes 6144 | tf_op jit(solution)/shard_map/gather | solution.py:121
  276.8 3.2 %all-to-all-start.2 = ((f32[1,4,128]{2,0,1:T(1,128)}), f32[1,4,128]{2,0,1:T(1,128)S(1)}, u32[]{:S(2)}, u32[]{:S(2)}) async-start(f32[1,4,128]{2,0,1:T(1,128)} %bitcast.20), calls=%async_computation.2 | async-start | bytes 4096 | tf_op jit(solution)/shard_map/all_to_all | solution.py:122
  280.1 3.6 %all-to-all-done.2 = f32[1,4,128]{2,0,1:T(1,128)S(1)} async-done(((f32[1,4,128]{2,0,1:T(1,128)}), f32[1,4,128]{2,0,1:T(1,128)S(1)}, u32[]{:S(2)}, u32[]{:S(2)}) %all-to-all-start.2) | async-done | bytes 2080 | tf_op jit(solution)/shard_map/all_to_all | solution.py:122
  283.7 3.5 %gather_fusion.1 = f32[512]{0:T(512)S(1)} fusion(f32[512]{0:T(512)S(1)} %bitcast.61, s32[1024]{0:T(1024)S(1)} %pad_clamp_fusion), kind=kCustom, calls=%fused_computation.1 | custom fusion | bytes 6144 | tf_op jit(solution)/shard_map/gather | solution.py:123
  (94 shorter events, 38.9 us)
Async XLA Ops:
  7.7 7.9 %all-to-all-start = ((s32[1,4,128]{2,0,1:T(1,128)}), s32[1,4,128]{2,0,1:T(1,128)S(1)}, u32[]{:S(2)}, u32[]{:S(2)}) async-start(s32[1,4,128]{2,0,1:T(1,128)} %bitcast.11), calls=%async_computation | async-start | bytes 4096 | tf_op jit(solution)/shard_map/all_to_all | solution.py:85
  15.6 7.0 %all-to-all-start.1 = ((f32[2,4,128]{2,0,1:T(2,128)}), f32[2,4,128]{2,0,1:T(2,128)S(1)}, u32[]{:S(2)}, u32[]{:S(2)}) async-start(f32[2,4,128]{2,0,1:T(2,128)} %copy.11), calls=%async_computation.1 | async-start | bytes 8192 | tf_op jit(solution)/shard_map/all_to_all | solution.py:84
  26.4 5.2 %copy-start.9 = (f32[256,256]{1,0:T(8,128)S(1)}, f32[256,256]{1,0:T(8,128)}, u32[]{:S(2)}) copy-start(f32[256,256]{1,0:T(8,128)} %param.6) | copy-start | bytes 786436
  27.6 17.0 %collective-permute-start = (f32[4,256,1]{2,1,0:T(8,128)}, f32[4,256,1]{2,1,0:T(8,128)S(1)}, u32[]{:S(2)}, u32[]{:S(2)}) collective-permute-start(f32[4,256,1]{2,1,0:T(8,128)} %get-tuple-element.26), channel_id=1, source_target_pairs={{0,4},{4,8},{8,12},{12,0},{1,5},{5,9},{9,13},{13,1},{2,6},{6,10},{... | collective-permute-start | bytes 12296 | tf_op jit(solution)/shard_map/ppermute | solution.py:18
  29.6 25.1 %collective-permute-start.1 = (f32[4,256,1]{2,1,0:T(8,128)}, f32[4,256,1]{2,1,0:T(8,128)S(1)}, u32[]{:S(2)}, u32[]{:S(2)}) collective-permute-start(f32[4,256,1]{2,1,0:T(8,128)} %get-tuple-element.27), channel_id=1, source_target_pairs={{4,0},{8,4},{12,8},{0,12},{5,1},{9,5},{13,9},{1,13},{6,2},{10,6},{... | collective-permute-start | bytes 12296 | tf_op jit(solution)/shard_map/ppermute | solution.py:21
  54.8 3.7 %collective-permute-start.2 = (f32[4,1,258]{2,1,0:T(1,128)S(1)}, f32[4,1,258]{2,1,0:T(1,128)S(1)}, u32[]{:S(2)}, u32[]{:S(2)}) collective-permute-start(f32[4,1,258]{2,1,0:T(1,128)S(1)} %get-tuple-element.14), channel_id=1, source_target_pairs={{0,2},{2,0},{1,3},{3,1},{4,6},{6,4},{5,7},{7,5},{8,10},{10,8},{9,1... | collective-permute-start | bytes 12392 | tf_op jit(solution)/shard_map/ppermute | solution.py:18
  54.9 3.6 %collective-permute-start.3 = (f32[4,1,258]{2,1,0:T(1,128)S(1)}, f32[4,1,258]{2,1,0:T(1,128)S(1)}, u32[]{:S(2)}, u32[]{:S(2)}) collective-permute-start(f32[4,1,258]{2,1,0:T(1,128)S(1)} %get-tuple-element.15), channel_id=1, source_target_pairs={{2,0},{0,2},{3,1},{1,3},{6,4},{4,6},{7,5},{5,7},{10,8},{8,10},{11,... | collective-permute-start | bytes 12392 | tf_op jit(solution)/shard_map/ppermute | solution.py:21
  59.2 3.8 %copy-start.3 = (f32[256,256]{1,0:T(8,128)S(1)}, f32[256,256]{1,0:T(8,128)}, u32[]{:S(2)}) copy-start(f32[256,256]{1,0:T(8,128)} %param.7) | copy-start | bytes 786436
  60.4 2.7 collective-permute-start.4
  61.8 3.4 %collective-permute-start.5 = (f32[1,256,256]{2,1,0:T(8,128)S(1)}, f32[1,256,256]{2,1,0:T(8,128)S(1)}, u32[]{:S(2)}, u32[]{:S(2)}) collective-permute-start(f32[1,256,256]{2,1,0:T(8,128)S(1)} %get-tuple-element.25), channel_id=1, source_target_pairs={{1,0},{3,2},{5,4},{7,6},{9,8},{11,10},{13,12},{15,14},{17,16},{19,... | collective-permute-start | bytes 786440 | tf_op jit(solution)/shard_map/ppermute | solution.py:21
  63.1 2.6 copy-start.5
  65.7 16.7 %collective-permute-start.6 = (f32[4,256,1]{2,1,0:T(8,128)S(1)}, f32[4,256,1]{2,1,0:T(8,128)S(1)}, u32[]{:S(2)}, u32[]{:S(2)}) collective-permute-start(f32[4,256,1]{2,1,0:T(8,128)S(1)} %get-tuple-element.22), channel_id=1, source_target_pairs={{0,4},{4,8},{8,12},{12,0},{1,5},{5,9},{9,13},{13,1},{2,6},{6,10},{... | collective-permute-start | bytes 12296 | tf_op jit(solution)/shard_map/ppermute | solution.py:18
  66.6 24.9 %collective-permute-start.7 = (f32[4,256,1]{2,1,0:T(8,128)S(1)}, f32[4,256,1]{2,1,0:T(8,128)S(1)}, u32[]{:S(2)}, u32[]{:S(2)}) collective-permute-start(f32[4,256,1]{2,1,0:T(8,128)S(1)} %get-tuple-element.23), channel_id=1, source_target_pairs={{4,0},{8,4},{12,8},{0,12},{5,1},{9,5},{13,9},{1,13},{6,2},{10,6},{... | collective-permute-start | bytes 12296 | tf_op jit(solution)/shard_map/ppermute | solution.py:21
  82.4 9.2 %copy-start.7 = (f32[4,256,1]{2,1,0:T(8,128)}, f32[4,256,1]{2,1,0:T(8,128)S(1)}, u32[]{:S(2)}) copy-start(f32[4,256,1]{2,1,0:T(8,128)S(1)} %collective-permute-done.6) | copy-start | bytes 12292
  92.4 7.9 %collective-permute-start.8 = (f32[4,1,258]{2,1,0:T(1,128)S(1)}, f32[4,1,258]{2,1,0:T(1,128)S(1)}, u32[]{:S(2)}, u32[]{:S(2)}) collective-permute-start(f32[4,1,258]{2,1,0:T(1,128)S(1)} %get-tuple-element.12), channel_id=1, source_target_pairs={{0,2},{2,0},{1,3},{3,1},{4,6},{6,4},{5,7},{7,5},{8,10},{10,8},{9,1... | collective-permute-start | bytes 12392 | tf_op jit(solution)/shard_map/ppermute | solution.py:18
  94.3 6.0 %collective-permute-start.9 = (f32[4,1,258]{2,1,0:T(1,128)S(1)}, f32[4,1,258]{2,1,0:T(1,128)S(1)}, u32[]{:S(2)}, u32[]{:S(2)}) collective-permute-start(f32[4,1,258]{2,1,0:T(1,128)S(1)} %get-tuple-element.13), channel_id=1, source_target_pairs={{2,0},{0,2},{3,1},{1,3},{6,4},{4,6},{7,5},{5,7},{10,8},{8,10},{11,... | collective-permute-start | bytes 12392 | tf_op jit(solution)/shard_map/ppermute | solution.py:21
  100.2 2.0 copy-start
  169.9 16.7 %collective-permute-start.10 = (f32[4,256,1]{2,1,0:T(8,128)S(1)}, f32[4,256,1]{2,1,0:T(8,128)S(1)}, u32[]{:S(2)}, u32[]{:S(2)}) collective-permute-start(f32[4,256,1]{2,1,0:T(8,128)S(1)} %get-tuple-element.20), channel_id=1, source_target_pairs={{0,4},{4,8},{8,12},{12,0},{1,5},{5,9},{9,13},{13,1},{2,6},{6,10},{... | collective-permute-start | bytes 12296 | tf_op jit(solution)/shard_map/ppermute | solution.py:18
  170.0 25.0 %collective-permute-start.11 = (f32[4,256,1]{2,1,0:T(8,128)S(1)}, f32[4,256,1]{2,1,0:T(8,128)S(1)}, u32[]{:S(2)}, u32[]{:S(2)}) collective-permute-start(f32[4,256,1]{2,1,0:T(8,128)S(1)} %get-tuple-element.21), channel_id=1, source_target_pairs={{4,0},{8,4},{12,8},{0,12},{5,1},{9,5},{13,9},{1,13},{6,2},{10,6},{... | collective-permute-start | bytes 12296 | tf_op jit(solution)/shard_map/ppermute | solution.py:21
  195.1 3.7 %collective-permute-start.12 = (f32[4,1,258]{2,1,0:T(1,128)S(1)}, f32[4,1,258]{2,1,0:T(1,128)S(1)}, u32[]{:S(2)}, u32[]{:S(2)}) collective-permute-start(f32[4,1,258]{2,1,0:T(1,128)S(1)} %get-tuple-element.10), channel_id=1, source_target_pairs={{0,2},{2,0},{1,3},{3,1},{4,6},{6,4},{5,7},{7,5},{8,10},{10,8},{9,1... | collective-permute-start | bytes 12392 | tf_op jit(solution)/shard_map/ppermute | solution.py:18
  195.1 3.7 %collective-permute-start.13 = (f32[4,1,258]{2,1,0:T(1,128)S(1)}, f32[4,1,258]{2,1,0:T(1,128)S(1)}, u32[]{:S(2)}, u32[]{:S(2)}) collective-permute-start(f32[4,1,258]{2,1,0:T(1,128)S(1)} %get-tuple-element.11), channel_id=1, source_target_pairs={{2,0},{0,2},{3,1},{1,3},{6,4},{4,6},{7,5},{5,7},{10,8},{8,10},{11,... | collective-permute-start | bytes 12392 | tf_op jit(solution)/shard_map/ppermute | solution.py:21
  199.5 6.0 %copy-start.4 = (f32[256,256]{1,0:T(8,128)S(1)}, f32[256,256]{1,0:T(8,128)}, u32[]{:S(2)}) copy-start(f32[256,256]{1,0:T(8,128)} %param.7) | copy-start | bytes 786436
  199.6 6.0 %copy-start.6 = (f32[256,256]{1,0:T(8,128)S(1)}, f32[256,256]{1,0:T(8,128)}, u32[]{:S(2)}) copy-start(f32[256,256]{1,0:T(8,128)} %copy-done.5) | copy-start | bytes 786436
  200.8 2.6 collective-permute-start.14
  202.1 3.4 %collective-permute-start.15 = (f32[1,256,256]{2,1,0:T(8,128)S(1)}, f32[1,256,256]{2,1,0:T(8,128)S(1)}, u32[]{:S(2)}, u32[]{:S(2)}) collective-permute-start(f32[1,256,256]{2,1,0:T(8,128)S(1)} %get-tuple-element.19), channel_id=1, source_target_pairs={{1,0},{3,2},{5,4},{7,6},{9,8},{11,10},{13,12},{15,14},{17,16},{19,... | collective-permute-start | bytes 786440 | tf_op jit(solution)/shard_map/ppermute | solution.py:21
  206.0 16.7 %collective-permute-start.16 = (f32[4,256,1]{2,1,0:T(8,128)S(1)}, f32[4,256,1]{2,1,0:T(8,128)S(1)}, u32[]{:S(2)}, u32[]{:S(2)}) collective-permute-start(f32[4,256,1]{2,1,0:T(8,128)S(1)} %get-tuple-element.16), channel_id=1, source_target_pairs={{0,4},{4,8},{8,12},{12,0},{1,5},{5,9},{9,13},{13,1},{2,6},{6,10},{... | collective-permute-start | bytes 12296 | tf_op jit(solution)/shard_map/ppermute | solution.py:18
  206.0 26.1 %collective-permute-start.17 = (f32[4,256,1]{2,1,0:T(8,128)S(1)}, f32[4,256,1]{2,1,0:T(8,128)S(1)}, u32[]{:S(2)}, u32[]{:S(2)}) collective-permute-start(f32[4,256,1]{2,1,0:T(8,128)S(1)} %get-tuple-element.17), channel_id=1, source_target_pairs={{4,0},{8,4},{12,8},{0,12},{5,1},{9,5},{13,9},{1,13},{6,2},{10,6},{... | collective-permute-start | bytes 12296 | tf_op jit(solution)/shard_map/ppermute | solution.py:21
  232.2 3.7 %collective-permute-start.18 = (f32[4,1,258]{2,1,0:T(1,128)S(1)}, f32[4,1,258]{2,1,0:T(1,128)S(1)}, u32[]{:S(2)}, u32[]{:S(2)}) collective-permute-start(f32[4,1,258]{2,1,0:T(1,128)S(1)} %get-tuple-element.8), channel_id=1, source_target_pairs={{0,2},{2,0},{1,3},{3,1},{4,6},{6,4},{5,7},{7,5},{8,10},{10,8},{9,1... | collective-permute-start | bytes 12392 | tf_op jit(solution)/shard_map/ppermute | solution.py:18
  234.2 4.4 %copy-start.1 = (f32[4,256,256]{2,1,0:T(8,128)S(1)}, f32[4,256,256]{2,1,0:T(8,128)}, u32[]{:S(2)}) copy-start(f32[4,256,256]{2,1,0:T(8,128)} %reshape.335) | copy-start | bytes 3145732
  234.2 3.6 %collective-permute-start.19 = (f32[4,1,258]{2,1,0:T(1,128)S(1)}, f32[4,1,258]{2,1,0:T(1,128)S(1)}, u32[]{:S(2)}, u32[]{:S(2)}) collective-permute-start(f32[4,1,258]{2,1,0:T(1,128)S(1)} %get-tuple-element.9), channel_id=1, source_target_pairs={{2,0},{0,2},{3,1},{1,3},{6,4},{4,6},{7,5},{5,7},{10,8},{8,10},{11,... | collective-permute-start | bytes 12392 | tf_op jit(solution)/shard_map/ppermute | solution.py:21
  272.0 4.8 %copy-start.2 = (f32[4,256,256]{2,1,0:T(8,128)}, f32[4,256,256]{2,1,0:T(8,128)S(1)}, u32[]{:S(2)}) copy-start(f32[4,256,256]{2,1,0:T(8,128)S(1)} %multiply_add_fusion) | copy-start | bytes 3145732
  276.8 6.9 %all-to-all-start.2 = ((f32[1,4,128]{2,0,1:T(1,128)}), f32[1,4,128]{2,0,1:T(1,128)S(1)}, u32[]{:S(2)}, u32[]{:S(2)}) async-start(f32[1,4,128]{2,0,1:T(1,128)} %bitcast.20), calls=%async_computation.2 | async-start | bytes 4096 | tf_op jit(solution)/shard_map/all_to_all | solution.py:122
  (1 other events, 0.8 us)
where the time goes:
time: 289 us; the launch traced here: 288 us
  waiting for transfers between devices  107 us (37%)
  blocking collectives  92.1 us (32%)
  starting transfers between devices  39.8 us (14%)
  other arithmetic  24.8 us (9%)
  local copies, waits for them, and re-layouts  18.2 us (6%)
  between operations  5.66 us (2%)
    psum x2, blocking collectives, square_sum(): return lax.psum(jnp.sum(vector * vector), ('lon', 'lat', 'tm'))  62 us
    ppermute x10, waiting for transfers between devices, extended_2(): lax.ppermute(lax.slice_in_dim(block, block.shape[dim] - width, None, axis...  56.2 us
    ppermute x10, waiting for transfers between devices, extended_2(): lax.ppermute(lax.slice_in_dim(block, 0, width, axis=dim), axis, backward)  43.3 us
    psum x1, blocking collectives, body(): lax.psum(jnp.sum(direction * applied), ('lon', 'lat', 'tm'))  30.1 us
    ppermute x10, starting transfers between devices, extended_2(): lax.ppermute(lax.slice_in_dim(block, 0, width, axis=dim), axis, backward)  19.3 us
    ppermute x10, starting transfers between devices, extended_2(): lax.ppermute(lax.slice_in_dim(block, block.shape[dim] - width, None, axis...  9.84 us
  transfers between devices with their start and end apart: 23, of which 19 were waited for; matrix products, arithmetic and copies ran while one was open for 3% of the time, Pallas kernels for 0%

commit v1 on v0

v1 whole, which is shorter than its diff:
```python
import functools

import jax
import jax.numpy as jnp
from jax import lax
from jax.experimental import pallas as pl
from jax.experimental.pallas import tpu as pltpu
from jax.sharding import PartitionSpec as P

HOURS = 8
BLOCK = 128
PAD = 8
ROWS = 64
LANES = 128
MESH = pl.DeviceIdType.MESH
F32 = jnp.float32
BF16 = jnp.bfloat16
NT = (((1,), (1,)), ((), ()))


def split(value):
    high = value.astype(BF16)
    return high, (value - high.astype(F32)).astype(BF16)


def dot(left, right, dims=None):
    if dims is None:
        return jnp.dot(left, right, preferred_element_type=F32)
    return lax.dot_general(left, right, dims, preferred_element_type=F32)


def fold(chunk):
    rows, cols = chunk.shape
    summed = jnp.sum(chunk.reshape(rows // 8, 8, cols), axis=0)
    total = summed[:, :LANES]
    for first in range(LANES, cols, LANES):
        total = total + summed[:, first : first + LANES]
    return total


def kernel(
    sizes,
    kappa_ref,
    tau_ref,
    value_ref,
    weight_ref,
    cell_ref,
    blocks_ref,
    field_ref,
    fit_ref,
    start_buf,
    image_buf,
    stiff_buf,
    couple_buf,
    second_buf,
    observed_buf,
    row_hot,
    lon_hot,
    slot_hot,
    station_out,
    station_in,
    back_out,
    back_in,
    edge_out,
    edge_in,
    columns,
    sum_out,
    sum_in,
    station_send,
    station_recv,
    back_send,
    back_recv,
    edge_send,
    edge_recv,
    plane_send,
    plane_recv,
    sum_send,
    sum_recv,
):
    n_lon, n_lat, n_tm, hours, lats, lons, stations, padded = sizes
    owners = n_lat * n_tm
    capacity = stations // owners
    slots = owners * padded
    members = n_lon * owners
    lon, lat, tm = lax.axis_index("lon"), lax.axis_index("lat"), lax.axis_index("tm")
    owner = lat * n_tm + tm
    member = lon * owners + owner
    edge_hour = jnp.where(tm == 0, hours - 1, 0)
    chunks = range(0, lats, ROWS)

    def place(index):
        return {
            "lon": lax.div(index, owners),
            "lat": lax.rem(lax.div(index, n_tm), n_lat),
            "tm": lax.rem(index, n_tm),
        }

    def place_owner(index):
        return {"lon": lon, "lat": lax.div(index, n_tm), "tm": lax.rem(index, n_tm)}

    barrier = pltpu.get_barrier_semaphore()

    def greet(step, carry):
        pl.semaphore_signal(
            barrier, inc=1, device_id=place(lax.rem(member + step, members)), device_id_type=MESH
        )
        return carry

    lax.fori_loop(1, members, greet, 0)

    live = lax.broadcasted_iota(jnp.int32, (1, stations), 1) < blocks_ref[0] * BLOCK
    weight = jnp.where(live, weight_ref[...], 0.0)
    lon_at, lat_at, hour_at = cell_ref[0:1, :], cell_ref[1:2, :], cell_ref[2:3, :]
    own_lat = jnp.zeros_like(lat_at)
    for band in range(1, n_lat):
        own_lat = own_lat + (lat_at >= band * lats).astype(jnp.int32)
    own_tm = jnp.zeros_like(lat_at)
    for group in range(1, n_tm):
        own_tm = own_tm + (hour_at >= group * hours).astype(jnp.int32)
    away = own_lat * n_tm + own_tm - owner
    away = jnp.where(away < 0, away + owners, away)
    row_at = (hour_at - own_tm * hours) * lats + lat_at - own_lat * lats
    col_at = lon_at - lon * lons
    kinds = max(16, owners)
    hot = lax.broadcasted_iota(jnp.int32, (kinds, stations), 0) == away
    earlier = lax.broadcasted_iota(jnp.int32, (stations, stations), 0) < lax.broadcasted_iota(
        jnp.int32, (stations, stations), 1
    )
    counts = dot(hot.astype(F32).astype(BF16), earlier.astype(F32).astype(BF16))
    rank = jnp.sum(jnp.where(hot, counts, 0.0), axis=0, keepdims=True).astype(jnp.int32)
    slot = away * padded + rank
    slot_hot[...] = (
        (lax.broadcasted_iota(jnp.int32, (slots, stations), 0) == slot).astype(F32).astype(BF16)
    )
    payload = jnp.concatenate(
        [
            weight,
            weight * value_ref[...],
            row_at.astype(F32),
            col_at.astype(F32),
            jnp.zeros((4, stations), F32),
        ],
        axis=0,
    )
    high, low = split(payload)
    both = dot(jnp.concatenate([high, low], axis=0), slot_hot[...], NT)
    packed = both[:8] + both[8:]
    for step in range(owners):
        chunk = packed[:, step * padded : (step + 1) * padded]
        if step == 0:
            station_in[owners - 1] = chunk
        else:
            station_out[step - 1] = chunk

    pl.semaphore_wait(barrier, members - 1)

    def station_copy(step):
        return pltpu.make_async_remote_copy(
            src_ref=station_out.at[step - 1],
            dst_ref=station_in.at[step - 1],
            send_sem=station_send.at[step - 1],
            recv_sem=station_recv.at[step - 1],
            device_id=place_owner(lax.rem(owner + step, owners)),
            device_id_type=MESH,
        )

    for step in range(1, owners):
        station_copy(step).start()
    for step in range(1, owners):
        station_copy(step).wait()

    arrived = jnp.concatenate([station_in[index] for index in range(owners)], axis=1)
    here_row = arrived[2:3].astype(jnp.int32)
    here_col = arrived[3:4].astype(jnp.int32)
    cells = hours * lats
    row_hot[...] = (
        (lax.broadcasted_iota(jnp.int32, (cells, slots), 0) == here_row).astype(F32).astype(BF16)
    )
    col_mask = lax.broadcasted_iota(jnp.int32, (lons, slots), 0) == here_col
    lon_hot[...] = col_mask.astype(F32).astype(BF16)

    def spread(quantity):
        high, low = split(jnp.where(col_mask, quantity, 0.0))
        return high, low

    weight_high, weight_low = spread(arrived[0:1])
    right_high, right_low = spread(arrived[1:2])

    for hour in range(hours):
        hot_rows = row_hot[hour * lats : (hour + 1) * lats, :]
        start_buf[hour, PAD : PAD + lats, :] = dot(hot_rows, right_high, NT) + dot(
            hot_rows, right_low, NT
        )

    lane = lax.broadcasted_iota(jnp.int32, (ROWS, lons), 1)
    lon_up, lon_down = lax.rem(lon + 1, n_lon), lax.rem(lon + n_lon - 1, n_lon)
    lat_up, lat_down = lax.rem(lat + 1, n_lat), lax.rem(lat + n_lat - 1, n_lat)
    lat_ways = 1 if n_lat == 2 else 2
    pair = lax.rem(tm + 1, n_tm)

    def edge_copies(phase, wide):
        copies = []
        ways = [(0, lon_up, lat), (0, lon_down, lat), (1, lon, lat_up), (1, lon, lat_down)]
        for across in range(2 if wide else 1):
            for way in range(2 + lat_ways):
                tile, to_lon, to_lat = ways[way]
                index = across * 4 + way
                copies.append(
                    pltpu.make_async_remote_copy(
                        src_ref=edge_out.at[phase, tile],
                        dst_ref=edge_in.at[phase, index],
                        send_sem=edge_send.at[phase, index],
                        recv_sem=edge_recv.at[phase, index],
                        device_id={"lon": to_lon, "lat": to_lat, "tm": pair if across else tm},
                        device_id_type=MESH,
                    )
                )
        return copies

    def plane_copy(ref, which):
        return pltpu.make_async_remote_copy(
            src_ref=ref.at[edge_hour, pl.ds(PAD, lats)],
            dst_ref=ref.at[hours, pl.ds(PAD, lats)],
            send_sem=plane_send.at[which],
            recv_sem=plane_recv.at[which],
            device_id={"lon": lon, "lat": lat, "tm": pair},
            device_id_type=MESH,
        )

    def send_edges(ref, phase, wide):
        last = [ref[hour, PAD : PAD + lats, lons - 1 : lons] for hour in range(hours)]
        first = [ref[hour, PAD : PAD + lats, 0:1] for hour in range(hours)]
        beside = jnp.concatenate(
            last + first + [jnp.zeros((lats, LANES - 2 * hours), F32)], axis=1
        )
        edge_out[phase, 0] = beside.T[: 2 * hours]
        edge_out[phase, 1] = jnp.concatenate(
            [ref[hour, PAD + lats - 1 : PAD + lats, :] for hour in range(hours)]
            + [ref[hour, PAD : PAD + 1, :] for hour in range(hours)],
            axis=0,
        )
        for copy in edge_copies(phase, wide):
            copy.start()

    def take_edges(ref, phase, wide):
        for copy in edge_copies(phase, wide):
            copy.wait()
        tiles = [edge_in[phase, index] for index in (0, 1)]
        if wide:
            tiles += [edge_in[phase, index] for index in (4, 5)]
        stacked = jnp.concatenate(
            tiles + [jnp.zeros((LANES - 2 * hours * len(tiles), lats), F32)], axis=0
        )
        columns[...] = stacked.T
        below = edge_in[phase, 2]
        above = edge_in[phase, 1 + lat_ways]
        for hour in range(hours):
            ref[hour, PAD - 1 : PAD, :] = jnp.where(lat == 0, 0.0, below[hour : hour + 1])
            ref[hour, PAD + lats : PAD + lats + 1, :] = jnp.where(
                lat == n_lat - 1, 0.0, above[hours + hour : hours + hour + 1]
            )
        if wide:
            below = edge_in[phase, 6]
            above = edge_in[phase, 5 + lat_ways]
            below = jnp.where(tm == 0, below[0:1], below[hours - 1 : hours])
            above = jnp.where(tm == 0, above[hours : hours + 1], above[2 * hours - 1 :])
            ref[hours, PAD - 1 : PAD, :] = jnp.where(lat == 0, 0.0, below)
            ref[hours, PAD + lats : PAD + lats + 1, :] = jnp.where(lat == n_lat - 1, 0.0, above)

    def stiffen(ref, hour, row):
        centre = ref[hour, PAD + row : PAD + row + ROWS, :]
        rows = slice(row, row + ROWS)
        if hour < hours:
            left = columns[rows, hour : hour + 1]
            right = columns[rows, 3 * hours + hour : 3 * hours + hour + 1]
        else:
            at = 4 * hours
            left = jnp.where(
                tm == 0, columns[rows, at : at + 1], columns[rows, at + hours - 1 : at + hours]
            )
            at = 7 * hours
            right = jnp.where(
                tm == 0, columns[rows, at : at + 1], columns[rows, at + hours - 1 : at + hours]
            )
        beside = (
            jnp.where(lane == 0, left, pltpu.roll(centre, 1, 1))
            + jnp.where(lane == lons - 1, right, pltpu.roll(centre, lons - 1, 1))
            + ref[hour, PAD + row - 1 : PAD + row - 1 + ROWS, :]
            + ref[hour, PAD + row + 1 : PAD + row + 1 + ROWS, :]
        )
        return (kappa_ref[rows, :] + 1.0) * centre - 0.25 * beside

    def couple(row):
        rows = slice(row, row + ROWS)
        tau = tau_ref[rows, :]
        inner = 1.0 + tau * tau
        plane = [stiff_buf[hour, rows, :] for hour in range(hours + 1)]
        for hour in range(hours):
            if hour == 0:
                below = jnp.where(tm == 0, 0.0, plane[hours])
                diagonal = jnp.where(tm == 0, 1.0, inner)
            else:
                below = plane[hour - 1]
                diagonal = inner
            if hour == hours - 1:
                above = jnp.where(tm == n_tm - 1, 0.0, plane[hours])
                diagonal = jnp.where(tm == n_tm - 1, 1.0, inner)
            else:
                above = plane[hour + 1]
            couple_buf[hour, PAD + row : PAD + row + ROWS, :] = diagonal * plane[hour] - tau * (
                below + above
            )

    def sum_start(which, partial):
        sum_out[which] = jnp.sum(partial, axis=0, keepdims=True)

        def send(step, carry):
            pltpu.make_async_remote_copy(
                src_ref=sum_out.at[which],
                dst_ref=sum_in.at[which, step - 1],
                send_sem=sum_send.at[which],
                recv_sem=sum_recv.at[which],
                device_id=place(lax.rem(member + step, members)),
                device_id_type=MESH,
            ).start()
            return carry

        if members <= 16:
            for step in range(1, members):
                send(step, 0)
        else:
            lax.fori_loop(1, members, send, 0)

    def sum_finish(which):
        pltpu.make_async_remote_copy(
            src_ref=sum_in.at[which],
            dst_ref=sum_in.at[which],
            send_sem=sum_send.at[which],
            recv_sem=sum_recv.at[which],
            device_id=place(lax.rem(member + 1, members)),
            device_id_type=MESH,
        ).wait()
        total = jnp.sum(sum_in[which], axis=0) + sum_out[which]
        return jnp.sum(total, axis=1, keepdims=True)

    def gather(ref):
        picked = jnp.zeros((1, slots), F32)
        for hour in range(hours):
            high, low = split(ref[hour, PAD : PAD + lats, :])
            found = dot(high, lon_hot[...]) + dot(low, lon_hot[...])
            hot_rows = row_hot[hour * lats : (hour + 1) * lats, :].astype(F32)
            picked = picked + jnp.sum(found * hot_rows, axis=0, keepdims=True)
        return picked

    plane_copy(start_buf, 0).start()
    send_edges(start_buf, 0, True)
    for hour in range(hours):
        hot_rows = row_hot[hour * lats : (hour + 1) * lats, :]
        observed_buf[hour] = dot(hot_rows, weight_high, NT) + dot(hot_rows, weight_low, NT)
    norm_part = jnp.zeros((8, LANES), F32)
    for hour in range(hours):
        for row in chunks:
            chunk = start_buf[hour, PAD + row : PAD + row + ROWS, :]
            norm_part = norm_part + fold(chunk * chunk)
    sum_start(0, norm_part)
    picked_start = gather(start_buf)

    def image(source, target, base, phase, which):
        plane_copy(source, which).wait()
        take_edges(source, phase, True)
        for hour in range(hours + 1):
            for row in chunks:
                stiff_buf[hour, row : row + ROWS, :] = stiffen(source, hour, row)
        for row in chunks:
            couple(row)
        send_edges(couple_buf, phase + 1, False)
        take_edges(couple_buf, phase + 1, False)
        part = jnp.zeros((8, LANES), F32)
        for hour in range(hours):
            for row in chunks:
                at = slice(base + row, base + row + ROWS)
                own = source[hour, PAD + row : PAD + row + ROWS, :]
                result = (
                    stiffen(couple_buf, hour, row)
                    + observed_buf[hour, row : row + ROWS, :] * own
                )
                target[hour, at, :] = result
                if which == 0:
                    part = part + fold(own * result)
        return part

    part = image(start_buf, image_buf, PAD, 0, 0)
    plane_copy(image_buf, 1).start()
    send_edges(image_buf, 2, True)
    sum_start(1, part)
    image(image_buf, second_buf, 0, 2, 1)

    norm = sum_finish(0)
    step_first = norm / sum_finish(1)
    part = jnp.zeros((8, LANES), F32)
    for hour in range(hours):
        for row in chunks:
            at = slice(PAD + row, PAD + row + ROWS)
            rest = start_buf[hour, at, :] - step_first * image_buf[hour, at, :]
            couple_buf[hour, at, :] = rest
            part = part + fold(rest * rest)
    sum_start(2, part)
    ratio = sum_finish(2)
    norm_next = ratio
    ratio = ratio / norm
    part = jnp.zeros((8, LANES), F32)
    for hour in range(hours):
        for row in chunks:
            at = slice(PAD + row, PAD + row + ROWS)
            applied = image_buf[hour, at, :]
            direction = couple_buf[hour, at, :] + ratio * start_buf[hour, at, :]
            turned = (
                applied - step_first * second_buf[hour, row : row + ROWS, :] + ratio * applied
            )
            couple_buf[hour, at, :] = direction
            part = part + fold(direction * turned)
    sum_start(3, part)

    picked = jnp.concatenate(
        [picked_start, gather(couple_buf), jnp.zeros((6, slots), F32)], axis=0
    )
    for step in range(1, owners + 1):
        chunk = picked[:, (step - 1) * padded : step * padded]
        if step == owners:
            back_in[0] = chunk
        else:
            back_out[step - 1] = chunk

    def back_copy(step):
        return pltpu.make_async_remote_copy(
            src_ref=back_out.at[step - 1],
            dst_ref=back_in.at[step],
            send_sem=back_send.at[step - 1],
            recv_sem=back_recv.at[step - 1],
            device_id=place_owner(lax.rem(owner + owners - step, owners)),
            device_id_type=MESH,
        )

    for step in range(1, owners):
        back_copy(step).start()
    for step in range(1, owners):
        back_copy(step).wait()
    returned = jnp.concatenate([back_in[index] for index in range(owners)], axis=1)
    high, low = split(returned)
    both = dot(jnp.concatenate([high, low], axis=0), slot_hot[...])
    fitted = both[:8] + both[8:]

    step_second = norm_next / sum_finish(3)
    for hour in range(hours):
        for row in chunks:
            at = slice(PAD + row, PAD + row + ROWS)
            field_ref[hour, row : row + ROWS, :] = (
                step_first * start_buf[hour, at, :] + step_second * couple_buf[hour, at, :]
            )
    fit_ref[...] = jnp.where(live, step_first * fitted[0:1] + step_second * fitted[1:2], 0.0)


def body(kappa_squared, time_coupling, station_value, station_weight, station_cell, slab_blocks):
    n_lon, n_lat, n_tm = (lax.axis_size(axis) for axis in ("lon", "lat", "tm"))
    lats, lons = kappa_squared.shape
    stations = station_value.shape[0]
    hours = HOURS // n_tm
    owners = n_lat * n_tm
    members = n_lon * owners
    padded = -(-(stations // owners) // LANES) * LANES
    slots = owners * padded
    sizes = (n_lon, n_lat, n_tm, hours, lats, lons, stations, padded)
    tall = lats + 2 * PAD
    vmem = pl.BlockSpec(memory_space=pltpu.VMEM)
    dma = pltpu.SemaphoreType.DMA
    field, fit = pl.pallas_call(
        functools.partial(kernel, sizes),
        out_shape=(
            jax.ShapeDtypeStruct((hours, lats, lons), F32),
            jax.ShapeDtypeStruct((1, stations), F32),
        ),
        in_specs=[vmem] * 5 + [pl.BlockSpec(memory_space=pltpu.SMEM)],
        out_specs=(vmem, vmem),
        scratch_shapes=[
            pltpu.VMEM((hours + 1, tall, lons), F32),
            pltpu.VMEM((hours + 1, tall, lons), F32),
            pltpu.VMEM((hours + 1, lats, lons), F32),
            pltpu.VMEM((hours, tall, lons), F32),
            pltpu.VMEM((hours, lats, lons), F32),
            pltpu.VMEM((hours, lats, lons), F32),
            pltpu.VMEM((hours * lats, slots), BF16),
            pltpu.VMEM((lons, slots), BF16),
            pltpu.VMEM((slots, stations), BF16),
            pltpu.VMEM((owners - 1, 8, padded), F32),
            pltpu.VMEM((owners, 8, padded), F32),
            pltpu.VMEM((owners - 1, 8, padded), F32),
            pltpu.VMEM((owners, 8, padded), F32),
            pltpu.VMEM((4, 2, 2 * hours, lats), F32),
            pltpu.VMEM((4, 8, 2 * hours, lats), F32),
            pltpu.VMEM((lats, LANES), F32),
            pltpu.VMEM((4, 1, LANES), F32),
            pltpu.VMEM((4, members - 1, 1, LANES), F32),
            dma((owners - 1,)),
            dma((owners - 1,)),
            dma((owners - 1,)),
            dma((owners - 1,)),
            dma((4, 8)),
            dma((4, 8)),
            dma((2,)),
            dma((2,)),
            dma((4,)),
            dma((4,)),
        ],
        compiler_params=pltpu.CompilerParams(
            collective_id=0, has_side_effects=True, vmem_limit_bytes=48 * 1024 * 1024
        ),
    )(
        kappa_squared,
        time_coupling,
        station_value.reshape(1, stations),
        station_weight.reshape(1, stations),
        station_cell,
        slab_blocks,
    )
    return field, fit.reshape(stations)


def solution(mesh):
    rows = P(("groups", "lon", "lat", "tm"))
    return jax.shard_map(
        body,
        mesh=mesh,
        in_specs=(
            P("lat", "lon"),
            P("lat", "lon"),
            rows,
            rows,
            P(None, ("groups", "lon", "lat", "tm")),
            P(("groups", "lon")),
        ),
        out_specs=(P(("groups", "tm"), "lat", "lon"), rows),
        check_vma=False,
    )
```

time: 289 us -> 46.5 us (0.16)
  waiting for transfers between devices: 107 us -> 0 us
  blocking collectives: 92.1 us -> 0 us
  Pallas kernels: 0 us -> 40.1 us
  starting transfers between devices: 39.8 us -> 0 us
  other arithmetic: 24.8 us -> 0 us
  local copies, waits for them, and re-layouts: 18.2 us -> 4.82 us
  between operations: 5.66 us -> 1.32 us
    ppermute x20 -> x0, waiting for transfers between devices: 99.5 us -> none  [the longest x10 56.2 us: extended_2(): lax.ppermute(lax.slice_in_dim(block, block.shape[dim] - width, None, axis...]
    psum x3 -> x0, blocking collectives: 92.1 us -> none  [the longest x2 62 us: square_sum(): return lax.psum(jnp.sum(vector * vector), ('lon', 'lat', 'tm'))]
    pallas_call x0 -> x1, Pallas kernels: none -> 40.1 us  [body(): pl.pallas_call(functools.partial(kernel, sizes), out_shape=(jax.ShapeDtyp...]
    ppermute x20 -> x0, starting transfers between devices: 29.1 us -> none  [the longest x10 19.3 us: extended_2(): lax.ppermute(lax.slice_in_dim(block, 0, width, axis=dim), axis, backward)]
    all_to_all x3 -> x0, starting transfers between devices: 10.7 us -> none  [the longest x1 4.21 us: body(): lax.all_to_all(cell_slots, ('lat', 'tm'), split_axis=1, concat_axis=1, ti...]
    gather x2 -> x0, local copies, waits for them, and re-layouts: 7.76 us -> none  [the longest x1 4.28 us: body(): picked = solution.reshape(-1)[cells_here][None, :]]
    all_to_all x3 -> x0, waiting for transfers between devices: 7.69 us -> none  [the longest x1 3.74 us: body(): lax.all_to_all(payload, ('lat', 'tm'), split_axis=1, concat_axis=1, tiled...]
    scatter-add x2 -> x0, other arithmetic: 7.22 us -> none  [the longest x1 3.7 us: body(): jnp.zeros(cell_total, jnp.float32).at[cells_here].add(arrived[1])]
  transfers between devices with their start and end apart: 23 -> 0, of which waited for: 19 -> 0; matrix products, arithmetic and copies ran while one was open for 3% -> 0% of each run, Pallas kernels for 0% -> 0%
where the time goes in v1:
time: 46.5 us; the launch traced here: 46.3 us
  Pallas kernels  40.1 us (86%)
  local copies, waits for them, and re-layouts  4.82 us (10%)
  between operations  1.32 us (3%)
    pallas_call x1, Pallas kernels, body(): pl.pallas_call(functools.partial(kernel, sizes), out_shape=(jax.ShapeDtyp...  40.1 us
    unnamed x12, local copies, waits for them, and re-layouts  4.82 us

profile of v1, /device:TPU:0, one launch (start us, length us, event | category | flops | bytes accessed | tf_op | source)
XLA Modules:
  0.0 46.3 jit_solution(16180957852572276278)
XLA Ops:
  0.6 0.0 copy-start.4
  1.3 0.0 copy-start.3
  1.3 0.0 copy-done.4
  1.3 0.7 %copy-done.3 = f32[512]{0:T(512)S(1)} copy-done((f32[512]{0:T(512)S(1)}, f32[512]{0:T(512)}, u32[]{:S(2)}) %copy-start.3) | copy-done | bytes 2072
  2.0 0.0 copy-start
  2.0 0.9 %copy-done = f32[256,256]{1,0:T(8,128)S(1)} copy-done((f32[256,256]{1,0:T(8,128)S(1)}, f32[256,256]{1,0:T(8,128)}, u32[]{:S(2)}) %copy-start) | copy-done | bytes 262168
  2.9 0.0 copy-start.1
  2.9 0.9 %copy-done.1 = f32[256,256]{1,0:T(8,128)S(1)} copy-done((f32[256,256]{1,0:T(8,128)S(1)}, f32[256,256]{1,0:T(8,128)}, u32[]{:S(2)}) %copy-start.1) | copy-done | bytes 262168
  3.9 0.0 copy-start.2
  3.9 0.7 %copy-done.2 = s32[3,512]{1,0:T(4,128)S(1)} copy-done((s32[3,512]{1,0:T(4,128)S(1)}, s32[3,512]{1,0:T(4,128)}, u32[]{:S(2)}) %copy-start.2) | copy-done | bytes 6168
  4.6 40.1 %shard_map.77 = (f32[4,256,256]{2,1,0:T(8,128)S(1)}, f32[1,512]{1,0:T(1,128)S(1)}) custom-call(f32[256,256]{1,0:T(8,128)S(1)} %copy-done, f32[256,256]{1,0:T(8,128)S(1)} %copy-done.1, f32[1,512]{1,0:T(1,128)S(1)} %bitcast.3, f32[1,512]{1,0:T(1,128)S(1)} %bitcast.4, s32[3,512]{1,0:T(4,128)S(1)} %copy-done.2, s32[1]{0:T(128)S(6)} %copy.10.blocks_ref), custom_call_target="tpu_custom_call" | custom-call | tf_op jit(solution)/shard_map/pallas_call | solution.py:476
  44.7 1.0 %copy.11 = f32[4,256,256]{2,1,0:T(8,128)} copy(f32[4,256,256]{2,1,0:T(8,128)S(1)} %get-tuple-element.8) | data formatting | bytes 2097152
  45.7 0.6 %copy.12 = f32[512]{0:T(512)} copy(f32[512]{0:T(512)S(1)} %bitcast.5) | data formatting | bytes 4096
Async XLA Ops:
  0.6 0.7 %copy-start.4 = (f32[512]{0:T(512)S(1)}, f32[512]{0:T(512)}, u32[]{:S(2)}) copy-start(f32[512]{0:T(512)} %param.9) | copy-start | bytes 6148
  1.3 0.7 %copy-start.3 = (f32[512]{0:T(512)S(1)}, f32[512]{0:T(512)}, u32[]{:S(2)}) copy-start(f32[512]{0:T(512)} %param.8) | copy-start | bytes 6148
  2.0 0.9 %copy-start = (f32[256,256]{1,0:T(8,128)S(1)}, f32[256,256]{1,0:T(8,128)}, u32[]{:S(2)}) copy-start(f32[256,256]{1,0:T(8,128)} %kappa_ref.1) | copy-start | bytes 786436
  2.9 0.9 %copy-start.1 = (f32[256,256]{1,0:T(8,128)S(1)}, f32[256,256]{1,0:T(8,128)}, u32[]{:S(2)}) copy-start(f32[256,256]{1,0:T(8,128)} %tau_ref.1) | copy-start | bytes 786436
  3.9 0.7 %copy-start.2 = (s32[3,512]{1,0:T(4,128)S(1)}, s32[3,512]{1,0:T(4,128)}, u32[]{:S(2)}) copy-start(s32[3,512]{1,0:T(4,128)} %cell_ref.1) | copy-start | bytes 18436

commit v2 on v1

--- a/solution.py
+++ b/solution.py
@@ -40,11 +40,11 @@
 
 def kernel(
     sizes,
-    kappa_ref,
-    tau_ref,
-    value_ref,
-    weight_ref,
-    cell_ref,
+    kappa_hbm,
+    tau_hbm,
+    value_hbm,
+    weight_hbm,
+    cell_hbm,
     blocks_ref,
     field_ref,
     fit_ref,
@@ -63,7 +63,15 @@
     back_in,
     edge_out,
     edge_in,
+    pair_in,
+    level_out,
+    level_in,
     columns,
+    kappa_ref,
+    tau_ref,
+    value_ref,
+    weight_ref,
+    cell_ref,
     sum_out,
     sum_in,
     station_send,
@@ -72,6 +80,11 @@
     back_recv,
     edge_send,
     edge_recv,
+    pair_send,
+    pair_recv,
+    level_send,
+    level_recv,
+    load_sem,
     plane_send,
     plane_recv,
     sum_send,
@@ -98,6 +111,20 @@
     def place_owner(index):
         return {"lon": lon, "lat": lax.div(index, n_tm), "tm": lax.rem(index, n_tm)}
 
+    loads = [
+        pltpu.make_async_copy(source, target, load_sem.at[index])
+        for index, (source, target) in enumerate(
+            [
+                (value_hbm, value_ref),
+                (weight_hbm, weight_ref),
+                (cell_hbm, cell_ref),
+                (kappa_hbm, kappa_ref),
+                (tau_hbm, tau_ref),
+            ]
+        )
+    ]
+    for load in loads:
+        load.start()
     barrier = pltpu.get_barrier_semaphore()
 
     def greet(step, carry):
@@ -107,6 +134,26 @@
         return carry
 
     lax.fori_loop(1, members, greet, 0)
+
+    for load in loads:
+        load.wait()
+    zeros = jnp.zeros((6, lats), F32)
+    coefficients = (kappa_ref, tau_ref)
+    sides = jnp.concatenate(
+        [ref[:, lons - 1 : lons] for ref in coefficients]
+        + [ref[:, 0:1] for ref in coefficients]
+        + [jnp.zeros((lats, LANES - 4), F32)],
+        axis=1,
+    ).T
+    level_out[0] = jnp.concatenate([sides[0:2], zeros], axis=0)
+    level_out[1] = jnp.concatenate([sides[2:4], zeros], axis=0)
+    zeros = jnp.zeros((6, lons), F32)
+    level_out[2] = jnp.concatenate([ref[lats - 1 : lats, :] for ref in coefficients] + [zeros], axis=0)
+    level_out[3] = jnp.concatenate([ref[0:1, :] for ref in coefficients] + [zeros], axis=0)
+    for ref in (start_buf, image_buf):
+        for hour in range(hours):
+            ref[hour, 0:PAD, :] = jnp.zeros((PAD, lons), F32)
+            ref[hour, PAD + lats :, :] = jnp.zeros((PAD, lons), F32)
 
     live = lax.broadcasted_iota(jnp.int32, (1, stations), 1) < blocks_ref[0] * BLOCK
     weight = jnp.where(live, weight_ref[...], 0.0)
@@ -152,6 +199,41 @@
         else:
             station_out[step - 1] = chunk
 
+    lane = lax.broadcasted_iota(jnp.int32, (ROWS, lons), 1)
+    lon_up, lon_down = lax.rem(lon + 1, n_lon), lax.rem(lon + n_lon - 1, n_lon)
+    lat_up, lat_down = lax.rem(lat + 1, n_lat), lax.rem(lat + n_lat - 1, n_lat)
+    pair = lax.rem(tm + 1, n_tm)
+    ways = (0, 1, 2, 4, 5) if n_lat == 2 else tuple(range(8))
+    slot_of = (0, 1, 2, 2, 4, 5, 4, 5) if n_lat == 2 else tuple(range(8))
+    upward = jnp.where(lat == 0, 2, 3) if n_lat == 2 else 2
+    targets = (
+        (0, lon_up, lat),
+        (1, lon_down, lat),
+        (upward, lon, lat_up),
+        (3, lon, lat_down),
+        (upward, lon_up, lat_up),
+        (upward, lon_down, lat_up),
+        (3, lon_up, lat_down),
+        (3, lon_down, lat_down),
+    )
+
+    def level_copies():
+        copies = []
+        for way in ways:
+            if way < 4:
+                tile, to_lon, to_lat = targets[way]
+                copies.append(
+                    pltpu.make_async_remote_copy(
+                        src_ref=level_out.at[tile],
+                        dst_ref=level_in.at[way],
+                        send_sem=level_send.at[way],
+                        recv_sem=level_recv.at[way],
+                        device_id={"lon": to_lon, "lat": to_lat, "tm": tm},
+                        device_id_type=MESH,
+                    )
+                )
+        return copies
+
     pl.semaphore_wait(barrier, members - 1)
 
     def station_copy(step):
@@ -166,6 +248,8 @@
 
     for step in range(1, owners):
         station_copy(step).start()
+    for copy in level_copies():
+        copy.start()
     for step in range(1, owners):
         station_copy(step).wait()
 
@@ -192,19 +276,12 @@
             hot_rows, right_low, NT
         )
 
-    lane = lax.broadcasted_iota(jnp.int32, (ROWS, lons), 1)
-    lon_up, lon_down = lax.rem(lon + 1, n_lon), lax.rem(lon + n_lon - 1, n_lon)
-    lat_up, lat_down = lax.rem(lat + 1, n_lat), lax.rem(lat + n_lat - 1, n_lat)
-    lat_ways = 1 if n_lat == 2 else 2
-    pair = lax.rem(tm + 1, n_tm)
-
-    def edge_copies(phase, wide):
+    def edge_copies(phase):
         copies = []
-        ways = [(0, lon_up, lat), (0, lon_down, lat), (1, lon, lat_up), (1, lon, lat_down)]
-        for across in range(2 if wide else 1):
-            for way in range(2 + lat_ways):
-                tile, to_lon, to_lat = ways[way]
-                index = across * 4 + way
+        for across in range(2):
+            for way in ways:
+                tile, to_lon, to_lat = targets[way]
+                index = across * 8 + way
                 copies.append(
                     pltpu.make_async_remote_copy(
                         src_ref=edge_out.at[phase, tile],
@@ -215,6 +292,16 @@
                         device_id_type=MESH,
                     )
                 )
+        copies.append(
+            pltpu.make_async_remote_copy(
+                src_ref=edge_out.at[phase],
+                dst_ref=pair_in.at[phase],
+                send_sem=pair_send.at[phase],
+                recv_sem=pair_recv.at[phase],
+                device_id={"lon": lon, "lat": lat, "tm": pair},
+                device_id_type=MESH,
+            )
+        )
         return copies
 
     def plane_copy(ref, which):
@@ -227,61 +314,135 @@
             device_id_type=MESH,
         )
 
-    def send_edges(ref, phase, wide):
-        last = [ref[hour, PAD : PAD + lats, lons - 1 : lons] for hour in range(hours)]
-        first = [ref[hour, PAD : PAD + lats, 0:1] for hour in range(hours)]
-        beside = jnp.concatenate(
-            last + first + [jnp.zeros((lats, LANES - 2 * hours), F32)], axis=1
-        )
-        edge_out[phase, 0] = beside.T[: 2 * hours]
-        edge_out[phase, 1] = jnp.concatenate(
-            [ref[hour, PAD + lats - 1 : PAD + lats, :] for hour in range(hours)]
-            + [ref[hour, PAD : PAD + 1, :] for hour in range(hours)],
+    def send_edges(ref, phase):
+        beside = [
+            ref[hour, PAD : PAD + lats, at : at + 1]
+            for at in (lons - 2, lons - 1, 0, 1)
+            for hour in range(hours)
+        ]
+        turned = jnp.concatenate(
+            beside + [jnp.zeros((lats, LANES - 4 * hours), F32)], axis=1
+        ).T
+        edge_out[phase, 0] = turned[: 2 * hours]
+        edge_out[phase, 1] = turned[2 * hours : 4 * hours]
+        for tile, first in ((2, lats - 2), (3, 0)):
+            edge_out[phase, tile] = jnp.concatenate(
+                [
+                    ref[hour, PAD + at : PAD + at + 1, :]
+                    for at in (first, first + 1)
+                    for hour in range(hours)
+                ],
+                axis=0,
+            )
+        for copy in edge_copies(phase):
+            copy.start()
+
+    def timeline(own, other, second):
+        at = second * hours
+        foreign = jnp.where(tm == 0, other[at : at + 1], other[at + hours - 1 : at + hours])
+        return jnp.concatenate(
+            [
+                jnp.where(tm == 0, 0.0, foreign),
+                own[at : at + hours],
+                jnp.where(tm == 0, foreign, 0.0),
+                jnp.zeros((8 - hours - 2, own.shape[1]), F32),
+            ],
             axis=0,
         )
-        for copy in edge_copies(phase, wide):
-            copy.start()
-
-    def take_edges(ref, phase, wide):
-        for copy in edge_copies(phase, wide):
+
+    hour_line = lax.broadcasted_iota(jnp.int32, (8, 1), 0)
+    at_edge = (hour_line == 1) & (tm == 0) | (hour_line == hours) & (tm == n_tm - 1)
+
+    def outer(far, near, inside, low, high, kappa, tau):
+        length = near.shape[1]
+        along = lax.broadcasted_iota(jnp.int32, (8, length), 1)
+        beside = (
+            far
+            + inside
+            + jnp.where(along == 0, low, pltpu.roll(near, 1, 1))
+            + jnp.where(along == length - 1, high, pltpu.roll(near, length - 1, 1))
+        )
+        stiff = (kappa + 1.0) * near - 0.25 * beside
+        diagonal = jnp.where(at_edge, 1.0, 1.0 + tau * tau)
+        return diagonal * stiff - tau * (pltpu.roll(stiff, 1, 0) + pltpu.roll(stiff, 7, 0))
+
+    def take_edges(ref, phase):
+        for copy in edge_copies(phase):
             copy.wait()
-        tiles = [edge_in[phase, index] for index in (0, 1)]
-        if wide:
-            tiles += [edge_in[phase, index] for index in (4, 5)]
-        stacked = jnp.concatenate(
-            tiles + [jnp.zeros((LANES - 2 * hours * len(tiles), lats), F32)], axis=0
-        )
-        columns[...] = stacked.T
-        below = edge_in[phase, 2]
-        above = edge_in[phase, 1 + lat_ways]
+        own = [edge_in[phase, slot_of[way]] for way in range(8)]
+        other = [edge_in[phase, 8 + slot_of[way]] for way in range(8)]
+        lines = {}
+        for way in range(8):
+            from_below = way in (0, 2, 4, 5)
+            lines[way] = timeline(own[way], other[way], 1 if from_below else 0)
+            if way < 4:
+                lines[way, "far"] = timeline(own[way], other[way], 0 if from_below else 1)
+        for way in (2, 4, 5):
+            lines[way] = jnp.where(lat == 0, 0.0, lines[way])
+        for way in (3, 6, 7):
+            lines[way] = jnp.where(lat == n_lat - 1, 0.0, lines[way])
+        within = [
+            timeline(edge_out[phase, tile], pair_in[phase, tile], second)
+            for tile, second in ((1, 0), (0, 1), (3, 0), (2, 1))
+        ]
+        corner = {
+            way: lines[way][:, lons - 1 : lons] if way in (4, 6) else lines[way][:, 0:1]
+            for way in (4, 5, 6, 7)
+        }
+        ends = {0: (4, 6), 1: (5, 7), 2: (4, 5), 3: (6, 7)}
+        coupled = []
+        for way in range(4):
+            level = level_in[slot_of[way]]
+            low, high = ends[way]
+            coupled.append(
+                outer(
+                    lines[way, "far"],
+                    lines[way],
+                    within[way],
+                    corner[low],
+                    corner[high],
+                    level[0:1],
+                    level[1:2],
+                )
+            )
+        coupled[2] = jnp.where(lat == 0, 0.0, coupled[2])
+        coupled[3] = jnp.where(lat == n_lat - 1, 0.0, coupled[3])
+        foreign = [
+            jnp.where(tm == 0, lines[way][hours + 1 : hours + 2], lines[way][0:1])
+            for way in range(4)
+        ]
+        columns[...] = jnp.concatenate(
+            [
+                lines[0][1 : hours + 1],
+                foreign[0],
+                jnp.zeros((7 - hours, lats), F32),
+                lines[1][1 : hours + 1],
+                foreign[1],
+                jnp.zeros((7 - hours, lats), F32),
+                coupled[0][1 : hours + 1],
+                coupled[1][1 : hours + 1],
+                jnp.zeros((LANES - 16 - 2 * hours, lats), F32),
+            ],
+            axis=0,
+        ).T
+        ref[hours, PAD - 1 : PAD, :] = foreign[2]
+        ref[hours, PAD + lats : PAD + lats + 1, :] = foreign[3]
         for hour in range(hours):
-            ref[hour, PAD - 1 : PAD, :] = jnp.where(lat == 0, 0.0, below[hour : hour + 1])
-            ref[hour, PAD + lats : PAD + lats + 1, :] = jnp.where(
-                lat == n_lat - 1, 0.0, above[hours + hour : hours + hour + 1]
+            at = slice(hour + 1, hour + 2)
+            stiff_buf[hour, 0:1, :] = stiff_buf[hour, 0:1, :] - 0.25 * lines[2][at]
+            stiff_buf[hour, lats - 1 : lats, :] = (
+                stiff_buf[hour, lats - 1 : lats, :] - 0.25 * lines[3][at]
             )
-        if wide:
-            below = edge_in[phase, 6]
-            above = edge_in[phase, 5 + lat_ways]
-            below = jnp.where(tm == 0, below[0:1], below[hours - 1 : hours])
-            above = jnp.where(tm == 0, above[hours : hours + 1], above[2 * hours - 1 :])
-            ref[hours, PAD - 1 : PAD, :] = jnp.where(lat == 0, 0.0, below)
-            ref[hours, PAD + lats : PAD + lats + 1, :] = jnp.where(lat == n_lat - 1, 0.0, above)
-
-    def stiffen(ref, hour, row):
+            couple_buf[hour, PAD - 1 : PAD, :] = coupled[2][at]
+            couple_buf[hour, PAD + lats : PAD + lats + 1, :] = coupled[3][at]
+
+    def stiffen(ref, hour, row, left=None, right=None):
         centre = ref[hour, PAD + row : PAD + row + ROWS, :]
         rows = slice(row, row + ROWS)
-        if hour < hours:
-            left = columns[rows, hour : hour + 1]
-            right = columns[rows, 3 * hours + hour : 3 * hours + hour + 1]
+        if left is None:
+            left, right = 0.0, 0.0
         else:
-            at = 4 * hours
-            left = jnp.where(
-                tm == 0, columns[rows, at : at + 1], columns[rows, at + hours - 1 : at + hours]
-            )
-            at = 7 * hours
-            right = jnp.where(
-                tm == 0, columns[rows, at : at + 1], columns[rows, at + hours - 1 : at + hours]
-            )
+            left, right = columns[rows, left : left + 1], columns[rows, right : right + 1]
         beside = (
             jnp.where(lane == 0, left, pltpu.roll(centre, 1, 1))
             + jnp.where(lane == lons - 1, right, pltpu.roll(centre, lons - 1, 1))
@@ -294,14 +455,22 @@
         rows = slice(row, row + ROWS)
         tau = tau_ref[rows, :]
         inner = 1.0 + tau * tau
-        plane = [stiff_buf[hour, rows, :] for hour in range(hours + 1)]
+        plane = []
         for hour in range(hours):
+            beside = jnp.where(
+                lane == 0,
+                columns[rows, hour : hour + 1],
+                jnp.where(lane == lons - 1, columns[rows, 8 + hour : 9 + hour], 0.0),
+            )
+            plane.append(stiff_buf[hour, rows, :] - 0.25 * beside)
+        plane.append(stiff_buf[hours, rows, :])
+        for hour in range(hours):
+            diagonal = inner
             if hour == 0:
                 below = jnp.where(tm == 0, 0.0, plane[hours])
                 diagonal = jnp.where(tm == 0, 1.0, inner)
             else:
                 below = plane[hour - 1]
-                diagonal = inner
             if hour == hours - 1:
                 above = jnp.where(tm == n_tm - 1, 0.0, plane[hours])
                 diagonal = jnp.where(tm == n_tm - 1, 1.0, inner)
@@ -353,7 +522,7 @@
         return picked
 
     plane_copy(start_buf, 0).start()
-    send_edges(start_buf, 0, True)
+    send_edges(start_buf, 0)
     for hour in range(hours):
         hot_rows = row_hot[hour * lats : (hour + 1) * lats, :]
         observed_buf[hour] = dot(hot_rows, weight_high, NT) + dot(hot_rows, weight_low, NT)
@@ -363,37 +532,43 @@
             chunk = start_buf[hour, PAD + row : PAD + row + ROWS, :]
             norm_part = norm_part + fold(chunk * chunk)
     sum_start(0, norm_part)
-    picked_start = gather(start_buf)
-
-    def image(source, target, base, phase, which):
-        plane_copy(source, which).wait()
-        take_edges(source, phase, True)
-        for hour in range(hours + 1):
+
+    def image(source, target, base, phase, meanwhile):
+        for hour in range(hours):
             for row in chunks:
                 stiff_buf[hour, row : row + ROWS, :] = stiffen(source, hour, row)
+        kept = meanwhile()
+        plane_copy(source, phase).wait()
+        take_edges(source, phase)
+        for row in chunks:
+            stiff_buf[hours, row : row + ROWS, :] = stiffen(source, hours, row, hours, 8 + hours)
         for row in chunks:
             couple(row)
-        send_edges(couple_buf, phase + 1, False)
-        take_edges(couple_buf, phase + 1, False)
         part = jnp.zeros((8, LANES), F32)
         for hour in range(hours):
             for row in chunks:
                 at = slice(base + row, base + row + ROWS)
                 own = source[hour, PAD + row : PAD + row + ROWS, :]
                 result = (
-                    stiffen(couple_buf, hour, row)
+                    stiffen(couple_buf, hour, row, 16 + hour, 16 + hours + hour)
                     + observed_buf[hour, row : row + ROWS, :] * own
                 )
                 target[hour, at, :] = result
-                if which == 0:
+                if phase == 0:
                     part = part + fold(own * result)
-        return part
-
-    part = image(start_buf, image_buf, PAD, 0, 0)
+        return part, kept
+
+    def first_meanwhile():
+        picked = gather(start_buf)
+        for copy in level_copies():
+            copy.wait()
+        return picked
+
+    part, picked_start = image(start_buf, image_buf, PAD, 0, first_meanwhile)
     plane_copy(image_buf, 1).start()
-    send_edges(image_buf, 2, True)
+    send_edges(image_buf, 1)
     sum_start(1, part)
-    image(image_buf, second_buf, 0, 2, 1)
+    image(image_buf, second_buf, 0, 1, lambda: None)
 
     norm = sum_finish(0)
     step_first = norm / sum_finish(1)
@@ -479,7 +654,7 @@
             jax.ShapeDtypeStruct((hours, lats, lons), F32),
             jax.ShapeDtypeStruct((1, stations), F32),
         ),
-        in_specs=[vmem] * 5 + [pl.BlockSpec(memory_space=pltpu.SMEM)],
+        in_specs=[pl.BlockSpec(memory_space=pl.ANY)] * 5 + [pl.BlockSpec(memory_space=pltpu.SMEM)],
         out_specs=(vmem, vmem),
         scratch_shapes=[
             pltpu.VMEM((hours + 1, tall, lons), F32),
@@ -495,17 +670,30 @@
             pltpu.VMEM((owners, 8, padded), F32),
             pltpu.VMEM((owners - 1, 8, padded), F32),
             pltpu.VMEM((owners, 8, padded), F32),
-            pltpu.VMEM((4, 2, 2 * hours, lats), F32),
-            pltpu.VMEM((4, 8, 2 * hours, lats), F32),
+            pltpu.VMEM((2, 4, 2 * hours, lats), F32),
+            pltpu.VMEM((2, 16, 2 * hours, lats), F32),
+            pltpu.VMEM((2, 4, 2 * hours, lats), F32),
+            pltpu.VMEM((4, 8, lats), F32),
+            pltpu.VMEM((4, 8, lats), F32),
             pltpu.VMEM((lats, LANES), F32),
+            pltpu.VMEM((lats, lons), F32),
+            pltpu.VMEM((lats, lons), F32),
+            pltpu.VMEM((1, stations), F32),
+            pltpu.VMEM((1, stations), F32),
+            pltpu.VMEM((3, stations), jnp.int32),
             pltpu.VMEM((4, 1, LANES), F32),
             pltpu.VMEM((4, members - 1, 1, LANES), F32),
             dma((owners - 1,)),
             dma((owners - 1,)),
             dma((owners - 1,)),
             dma((owners - 1,)),
-            dma((4, 8)),
-            dma((4, 8)),
+            dma((2, 16)),
+            dma((2, 16)),
+            dma((2,)),
+            dma((2,)),
+            dma((4,)),
+            dma((4,)),
+            dma((5,)),
             dma((2,)),
             dma((2,)),
             dma((4,)),

time: 46.5 us -> 39.3 us (0.85)
  Pallas kernels: 40.1 us -> 32.8 us
    pallas_call x1, Pallas kernels: 40.1 us -> 32.8 us  [body(): pl.pallas_call(functools.partial(kernel, sizes), out_shape=(jax.ShapeDtyp...]
where the time goes in v2:
time: 39.3 us; the launch traced here: 39 us
  Pallas kernels  32.8 us (83%)
  local copies, waits for them, and re-layouts  4.82 us (12%)
  between operations  1.32 us (3%)
    pallas_call x1, Pallas kernels, body(): pl.pallas_call(functools.partial(kernel, sizes), out_shape=(jax.ShapeDtyp...  32.8 us
    unnamed x12, local copies, waits for them, and re-layouts  4.82 us

profile of v2, /device:TPU:0, one launch (start us, length us, event | category | flops | bytes accessed | tf_op | source)
XLA Modules:
  0.0 39.0 jit_solution(4124063989120124788)
XLA Ops:
  0.6 0.0 copy-start.4
  1.3 0.0 copy-start.3
  1.3 0.0 copy-done.4
  1.3 0.7 %copy-done.3 = f32[512]{0:T(512)S(1)} copy-done((f32[512]{0:T(512)S(1)}, f32[512]{0:T(512)}, u32[]{:S(2)}) %copy-start.3) | copy-done | bytes 2072
  2.0 0.0 copy-start
  2.0 0.9 %copy-done = f32[256,256]{1,0:T(8,128)S(1)} copy-done((f32[256,256]{1,0:T(8,128)S(1)}, f32[256,256]{1,0:T(8,128)}, u32[]{:S(2)}) %copy-start) | copy-done | bytes 262168
  2.9 0.0 copy-start.1
  2.9 0.9 %copy-done.1 = f32[256,256]{1,0:T(8,128)S(1)} copy-done((f32[256,256]{1,0:T(8,128)S(1)}, f32[256,256]{1,0:T(8,128)}, u32[]{:S(2)}) %copy-start.1) | copy-done | bytes 262168
  3.9 0.0 copy-start.2
  3.9 0.7 %copy-done.2 = s32[3,512]{1,0:T(4,128)S(1)} copy-done((s32[3,512]{1,0:T(4,128)S(1)}, s32[3,512]{1,0:T(4,128)}, u32[]{:S(2)}) %copy-start.2) | copy-done | bytes 6168
  4.6 32.8 %shard_map.77 = (f32[4,256,256]{2,1,0:T(8,128)S(1)}, f32[1,512]{1,0:T(1,128)S(1)}) custom-call(f32[256,256]{1,0:T(8,128)S(1)} %copy-done, f32[256,256]{1,0:T(8,128)S(1)} %copy-done.1, f32[1,512]{1,0:T(1,128)S(1)} %bitcast.3, f32[1,512]{1,0:T(1,128)S(1)} %bitcast.4, s32[3,512]{1,0:T(4,128)S(1)} %copy-done.2, s32[1]{0:T(128)S(6)} %copy.10.blocks_ref), custom_call_target="tpu_custom_call" | custom-call | tf_op jit(solution)/shard_map/pallas_call | solution.py:651
  37.4 1.0 %copy.11 = f32[4,256,256]{2,1,0:T(8,128)} copy(f32[4,256,256]{2,1,0:T(8,128)S(1)} %get-tuple-element.8) | data formatting | bytes 2097152
  38.4 0.6 %copy.12 = f32[512]{0:T(512)} copy(f32[512]{0:T(512)S(1)} %bitcast.5) | data formatting | bytes 4096
Async XLA Ops:
  0.6 0.7 %copy-start.4 = (f32[512]{0:T(512)S(1)}, f32[512]{0:T(512)}, u32[]{:S(2)}) copy-start(f32[512]{0:T(512)} %param.9) | copy-start | bytes 6148
  1.3 0.7 %copy-start.3 = (f32[512]{0:T(512)S(1)}, f32[512]{0:T(512)}, u32[]{:S(2)}) copy-start(f32[512]{0:T(512)} %param.8) | copy-start | bytes 6148
  2.0 0.9 %copy-start = (f32[256,256]{1,0:T(8,128)S(1)}, f32[256,256]{1,0:T(8,128)}, u32[]{:S(2)}) copy-start(f32[256,256]{1,0:T(8,128)} %kappa_hbm.1) | copy-start | bytes 786436
  2.9 0.9 %copy-start.1 = (f32[256,256]{1,0:T(8,128)S(1)}, f32[256,256]{1,0:T(8,128)}, u32[]{:S(2)}) copy-start(f32[256,256]{1,0:T(8,128)} %tau_hbm.1) | copy-start | bytes 786436
  3.9 0.7 %copy-start.2 = (s32[3,512]{1,0:T(4,128)S(1)}, s32[3,512]{1,0:T(4,128)}, u32[]{:S(2)}) copy-start(s32[3,512]{1,0:T(4,128)} %cell_hbm.1) | copy-start | bytes 18436

commit v3 on v2

--- a/solution.py
+++ b/solution.py
@@ -12,6 +12,7 @@
 PAD = 8
 ROWS = 64
 LANES = 128
+VMEM_LIMIT = 62 * 1024 * 1024
 MESH = pl.DeviceIdType.MESH
 F32 = jnp.float32
 BF16 = jnp.bfloat16
@@ -97,16 +98,30 @@
     members = n_lon * owners
     lon, lat, tm = lax.axis_index("lon"), lax.axis_index("lat"), lax.axis_index("tm")
     owner = lat * n_tm + tm
-    member = lon * owners + owner
     edge_hour = jnp.where(tm == 0, hours - 1, 0)
     chunks = range(0, lats, ROWS)
 
-    def place(index):
-        return {
-            "lon": lax.div(index, owners),
-            "lat": lax.rem(lax.div(index, n_tm), n_lat),
-            "tm": lax.rem(index, n_tm),
-        }
+    def others(act):
+        def at_lon(step_lon, skip):
+            to_lon = lon + step_lon
+            to_lon = jnp.where(to_lon >= n_lon, to_lon - n_lon, to_lon)
+            for step_lat in range(n_lat):
+                to_lat = lat + step_lat
+                to_lat = jnp.where(to_lat >= n_lat, to_lat - n_lat, to_lat)
+                for step_tm in range(n_tm):
+                    if skip and step_lat == 0 and step_tm == 0:
+                        continue
+                    to_tm = tm + step_tm
+                    to_tm = jnp.where(to_tm >= n_tm, to_tm - n_tm, to_tm)
+                    slot = (step_lon * n_lat + step_lat) * n_tm + step_tm - 1
+                    act({"lon": to_lon, "lat": to_lat, "tm": to_tm}, slot)
+
+        at_lon(0, True)
+        if n_lon <= 4:
+            for step_lon in range(1, n_lon):
+                at_lon(step_lon, False)
+        else:
+            lax.fori_loop(1, n_lon, lambda step, carry: (at_lon(step, False), carry)[1], 0)
 
     def place_owner(index):
         return {"lon": lon, "lat": lax.div(index, n_tm), "tm": lax.rem(index, n_tm)}
@@ -127,13 +142,10 @@
         load.start()
     barrier = pltpu.get_barrier_semaphore()
 
-    def greet(step, carry):
-        pl.semaphore_signal(
-            barrier, inc=1, device_id=place(lax.rem(member + step, members)), device_id_type=MESH
-        )
-        return carry
-
-    lax.fori_loop(1, members, greet, 0)
+    def greet(place, slot):
+        pl.semaphore_signal(barrier, inc=1, device_id=place, device_id_type=MESH)
+
+    others(greet)
 
     for load in loads:
         load.wait()
@@ -282,10 +294,14 @@
             for way in ways:
                 tile, to_lon, to_lat = targets[way]
                 index = across * 8 + way
+                source, target = edge_out.at[phase, tile], edge_in.at[phase, index]
+                if way >= 4:
+                    half = pl.ds(lons - LANES if way in (4, 6) else 0, LANES)
+                    source, target = source.at[:, half], target.at[:, half]
                 copies.append(
                     pltpu.make_async_remote_copy(
-                        src_ref=edge_out.at[phase, tile],
-                        dst_ref=edge_in.at[phase, index],
+                        src_ref=source,
+                        dst_ref=target,
                         send_sem=edge_send.at[phase, index],
                         recv_sem=edge_recv.at[phase, index],
                         device_id={"lon": to_lon, "lat": to_lat, "tm": pair if across else tm},
@@ -369,8 +385,12 @@
     def take_edges(ref, phase):
         for copy in edge_copies(phase):
             copy.wait()
-        own = [edge_in[phase, slot_of[way]] for way in range(8)]
-        other = [edge_in[phase, 8 + slot_of[way]] for way in range(8)]
+        span = {way: slice(lons - LANES, lons) for way in (4, 6)} | {
+            way: slice(0, LANES) for way in (5, 7)
+        }
+        every = slice(0, lons)
+        own = [edge_in[phase, slot_of[way], :, span.get(way, every)] for way in range(8)]
+        other = [edge_in[phase, 8 + slot_of[way], :, span.get(way, every)] for way in range(8)]
         lines = {}
         for way in range(8):
             from_below = way in (0, 2, 4, 5)
@@ -386,7 +406,7 @@
             for tile, second in ((1, 0), (0, 1), (3, 0), (2, 1))
         ]
         corner = {
-            way: lines[way][:, lons - 1 : lons] if way in (4, 6) else lines[way][:, 0:1]
+            way: lines[way][:, LANES - 1 :] if way in (4, 6) else lines[way][:, 0:1]
             for way in (4, 5, 6, 7)
         }
         ends = {0: (4, 6), 1: (5, 7), 2: (4, 5), 3: (6, 7)}
@@ -483,22 +503,17 @@
     def sum_start(which, partial):
         sum_out[which] = jnp.sum(partial, axis=0, keepdims=True)
 
-        def send(step, carry):
+        def send(place, slot):
             pltpu.make_async_remote_copy(
                 src_ref=sum_out.at[which],
-                dst_ref=sum_in.at[which, step - 1],
+                dst_ref=sum_in.at[which, slot],
                 send_sem=sum_send.at[which],
                 recv_sem=sum_recv.at[which],
-                device_id=place(lax.rem(member + step, members)),
+                device_id=place,
                 device_id_type=MESH,
             ).start()
-            return carry
-
-        if members <= 16:
-            for step in range(1, members):
-                send(step, 0)
-        else:
-            lax.fori_loop(1, members, send, 0)
+
+        others(send)
 
     def sum_finish(which):
         pltpu.make_async_remote_copy(
@@ -506,7 +521,7 @@
             dst_ref=sum_in.at[which],
             send_sem=sum_send.at[which],
             recv_sem=sum_recv.at[which],
-            device_id=place(lax.rem(member + 1, members)),
+            device_id={"lon": lon, "lat": lat, "tm": pair},
             device_id_type=MESH,
         ).wait()
         total = jnp.sum(sum_in[which], axis=0) + sum_out[which]
@@ -580,21 +595,6 @@
             couple_buf[hour, at, :] = rest
             part = part + fold(rest * rest)
     sum_start(2, part)
-    ratio = sum_finish(2)
-    norm_next = ratio
-    ratio = ratio / norm
-    part = jnp.zeros((8, LANES), F32)
-    for hour in range(hours):
-        for row in chunks:
-            at = slice(PAD + row, PAD + row + ROWS)
-            applied = image_buf[hour, at, :]
-            direction = couple_buf[hour, at, :] + ratio * start_buf[hour, at, :]
-            turned = (
-                applied - step_first * second_buf[hour, row : row + ROWS, :] + ratio * applied
-            )
-            couple_buf[hour, at, :] = direction
-            part = part + fold(direction * turned)
-    sum_start(3, part)
 
     picked = jnp.concatenate(
         [picked_start, gather(couple_buf), jnp.zeros((6, slots), F32)], axis=0
@@ -618,6 +618,25 @@
 
     for step in range(1, owners):
         back_copy(step).start()
+    for hour in range(hours):
+        for row in chunks:
+            at = slice(row, row + ROWS)
+            second_buf[hour, at, :] = (
+                image_buf[hour, PAD + row : PAD + row + ROWS, :]
+                - step_first * second_buf[hour, at, :]
+            )
+    norm_next = sum_finish(2)
+    ratio = norm_next / norm
+    part = jnp.zeros((8, LANES), F32)
+    for hour in range(hours):
+        for row in chunks:
+            at = slice(PAD + row, PAD + row + ROWS)
+            direction = couple_buf[hour, at, :] + ratio * start_buf[hour, at, :]
+            turned = second_buf[hour, row : row + ROWS, :] + ratio * image_buf[hour, at, :]
+            couple_buf[hour, at, :] = direction
+            part = part + fold(direction * turned)
+    sum_start(3, part)
+
     for step in range(1, owners):
         back_copy(step).wait()
     returned = jnp.concatenate([back_in[index] for index in range(owners)], axis=1)
@@ -632,7 +651,8 @@
             field_ref[hour, row : row + ROWS, :] = (
                 step_first * start_buf[hour, at, :] + step_second * couple_buf[hour, at, :]
             )
-    fit_ref[...] = jnp.where(live, step_first * fitted[0:1] + step_second * fitted[1:2], 0.0)
+    fitted_at = step_first * fitted[0:1] + step_second * (fitted[1:2] + ratio * fitted[0:1])
+    fit_ref[...] = jnp.where(live, fitted_at, 0.0)
 
 
 def body(kappa_squared, time_coupling, station_value, station_weight, station_cell, slab_blocks):
@@ -700,7 +720,7 @@
             dma((4,)),
         ],
         compiler_params=pltpu.CompilerParams(
-            collective_id=0, has_side_effects=True, vmem_limit_bytes=48 * 1024 * 1024
+            collective_id=0, has_side_effects=True, vmem_limit_bytes=VMEM_LIMIT
         ),
     )(
         kappa_squared,

time: 39.3 us -> 37.8 us (0.962)
  local copies, waits for them, and re-layouts: 4.82 us -> 2.87 us
  Pallas kernels: 32.8 us -> 33.4 us
    unnamed x12 -> x4, local copies, waits for them, and re-layouts: 4.82 us -> 2.87 us
    pallas_call x1, Pallas kernels: 32.8 us -> 33.4 us  [body(): pl.pallas_call(functools.partial(kernel, sizes), out_shape=(jax.ShapeDtyp...]
where the time goes in v3:
time: 37.8 us; the launch traced here: 37.6 us
  Pallas kernels  33.4 us (88%)
  local copies, waits for them, and re-layouts  2.87 us (8%)
  between operations  1.29 us (3%)
    pallas_call x1, Pallas kernels, body(): pl.pallas_call(functools.partial(kernel, sizes), out_shape=(jax.ShapeDtyp...  33.4 us
    unnamed x4, local copies, waits for them, and re-layouts  2.87 us

profile of v3, /device:TPU:0, one launch (start us, length us, event | category | flops | bytes accessed | tf_op | source)
XLA Modules:
  0.0 37.6 jit_solution(7523508488316624739)
XLA Ops:
  1.3 33.4 %shard_map.77 = (f32[4,256,256]{2,1,0:T(8,128)}, f32[1,512]{1,0:T(1,128)}) custom-call(f32[256,256]{1,0:T(8,128)} %kappa_hbm.1, f32[256,256]{1,0:T(8,128)} %tau_hbm.1, f32[1,512]{1,0:T(1,128)} %bitcast.3, f32[1,512]{1,0:T(1,128)} %bitcast.4, s32[3,512]{1,0:T(4,128)} %cell_hbm.1, s32[1]{0:T(128)S(6)} %copy.10.blocks_ref), custom_call_target="tpu_custom_call" | custom-call | tf_op jit(solution)/shard_map/pallas_call | solution.py:671
  34.7 0.0 copy-start
  34.7 2.3 %copy.11 = f32[4,256,256]{2,1,0:T(8,128)} copy(f32[4,256,256]{2,1,0:T(8,128)} %get-tuple-element.8) | data formatting | bytes 2097152
  37.0 0.0 copy-done
  37.0 0.6 %copy.12 = f32[512]{0:T(512)} copy(f32[512]{0:T(512)S(1)} %bitcast.5) | data formatting | bytes 4096
Async XLA Ops:
  34.7 2.3 %copy-start = (f32[1,512]{1,0:T(1,128)S(1)}, f32[1,512]{1,0:T(1,128)}, u32[]{:S(2)}) copy-start(f32[1,512]{1,0:T(1,128)} %get-tuple-element.5) | copy-start | bytes 6148

commit v4 on v3

--- a/solution.py
+++ b/solution.py
@@ -12,7 +12,7 @@
 PAD = 8
 ROWS = 64
 LANES = 128
-VMEM_LIMIT = 62 * 1024 * 1024
+VMEM_LIMIT = 60 * 1024 * 1024
 MESH = pl.DeviceIdType.MESH
 F32 = jnp.float32
 BF16 = jnp.bfloat16
@@ -671,8 +671,8 @@
     field, fit = pl.pallas_call(
         functools.partial(kernel, sizes),
         out_shape=(
-            jax.ShapeDtypeStruct((hours, lats, lons), F32),
-            jax.ShapeDtypeStruct((1, stations), F32),
+            pltpu.VMEM((hours, lats, lons), F32),
+            pltpu.VMEM((1, stations), F32),
         ),
         in_specs=[pl.BlockSpec(memory_space=pl.ANY)] * 5 + [pl.BlockSpec(memory_space=pltpu.SMEM)],
         out_specs=(vmem, vmem),

time: 37.8 us -> 35.4 us (0.937)
  local copies, waits for them, and re-layouts: 2.87 us -> 1.55 us
  Pallas kernels: 33.4 us -> 32.4 us
    unnamed x4 -> x2, local copies, waits for them, and re-layouts: 2.87 us -> 1.55 us
    pallas_call x1, Pallas kernels: 33.4 us -> 32.4 us  [body(): pl.pallas_call(functools.partial(kernel, sizes), out_shape=(pltpu.VMEM((h...]
where the time goes in v4:
time: 35.4 us; the launch traced here: 35.3 us
  Pallas kernels  32.4 us (92%)
  local copies, waits for them, and re-layouts  1.55 us (4%)
  between operations  1.29 us (4%)
    pallas_call x1, Pallas kernels, body(): pl.pallas_call(functools.partial(kernel, sizes), out_shape=(pltpu.VMEM((h...  32.4 us
    unnamed x2, local copies, waits for them, and re-layouts  1.55 us

profile of v4, /device:TPU:0, one launch (start us, length us, event | category | flops | bytes accessed | tf_op | source)
XLA Modules:
  0.0 35.3 jit_solution(3221161610199051752)
XLA Ops:
  1.3 32.4 %shard_map.77 = (f32[4,256,256]{2,1,0:T(8,128)S(1)}, f32[1,512]{1,0:T(1,128)S(1)}) custom-call(f32[256,256]{1,0:T(8,128)} %kappa_hbm.1, f32[256,256]{1,0:T(8,128)} %tau_hbm.1, f32[1,512]{1,0:T(1,128)} %bitcast.4, f32[1,512]{1,0:T(1,128)} %bitcast.5, s32[3,512]{1,0:T(4,128)} %cell_hbm.1, s32[1]{0:T(128)S(6)} %copy.12.blocks_ref), custom_call_target="tpu_custom_call" | custom-call | tf_op jit(solution)/shard_map/pallas_call | solution.py:671
  33.7 1.0 %copy.10 = f32[4,256,256]{2,1,0:T(8,128)} copy(f32[4,256,256]{2,1,0:T(8,128)S(1)} %get-tuple-element.6) | data formatting | bytes 2097152
  34.7 0.6 %copy.11 = f32[512]{0:T(512)} copy(f32[512]{0:T(512)S(1)} %bitcast.3) | data formatting | bytes 4096

commit v5 on v4

--- a/solution.py
+++ b/solution.py
@@ -147,26 +147,8 @@
 
     others(greet)
 
-    for load in loads:
+    for load in loads[:3]:
         load.wait()
-    zeros = jnp.zeros((6, lats), F32)
-    coefficients = (kappa_ref, tau_ref)
-    sides = jnp.concatenate(
-        [ref[:, lons - 1 : lons] for ref in coefficients]
-        + [ref[:, 0:1] for ref in coefficients]
-        + [jnp.zeros((lats, LANES - 4), F32)],
-        axis=1,
-    ).T
-    level_out[0] = jnp.concatenate([sides[0:2], zeros], axis=0)
-    level_out[1] = jnp.concatenate([sides[2:4], zeros], axis=0)
-    zeros = jnp.zeros((6, lons), F32)
-    level_out[2] = jnp.concatenate([ref[lats - 1 : lats, :] for ref in coefficients] + [zeros], axis=0)
-    level_out[3] = jnp.concatenate([ref[0:1, :] for ref in coefficients] + [zeros], axis=0)
-    for ref in (start_buf, image_buf):
-        for hour in range(hours):
-            ref[hour, 0:PAD, :] = jnp.zeros((PAD, lons), F32)
-            ref[hour, PAD + lats :, :] = jnp.zeros((PAD, lons), F32)
-
     live = lax.broadcasted_iota(jnp.int32, (1, stations), 1) < blocks_ref[0] * BLOCK
     weight = jnp.where(live, weight_ref[...], 0.0)
     lon_at, lat_at, hour_at = cell_ref[0:1, :], cell_ref[1:2, :], cell_ref[2:3, :]
@@ -260,6 +242,25 @@
 
     for step in range(1, owners):
         station_copy(step).start()
+    for load in loads[3:]:
+        load.wait()
+    zeros = jnp.zeros((6, lats), F32)
+    coefficients = (kappa_ref, tau_ref)
+    sides = jnp.concatenate(
+        [ref[:, lons - 1 : lons] for ref in coefficients]
+        + [ref[:, 0:1] for ref in coefficients]
+        + [jnp.zeros((lats, LANES - 4), F32)],
+        axis=1,
+    ).T
+    level_out[0] = jnp.concatenate([sides[0:2], zeros], axis=0)
+    level_out[1] = jnp.concatenate([sides[2:4], zeros], axis=0)
+    zeros = jnp.zeros((6, lons), F32)
+    level_out[2] = jnp.concatenate([ref[lats - 1 : lats, :] for ref in coefficients] + [zeros], axis=0)
+    level_out[3] = jnp.concatenate([ref[0:1, :] for ref in coefficients] + [zeros], axis=0)
+    for ref in (start_buf, image_buf):
+        for hour in range(hours):
+            ref[hour, 0:PAD, :] = jnp.zeros((PAD, lons), F32)
+            ref[hour, PAD + lats :, :] = jnp.zeros((PAD, lons), F32)
     for copy in level_copies():
         copy.start()
     for step in range(1, owners):

time: 35.4 us -> 35.4 us (level)
  no operation moved by 1% of the time
where the time goes in v5:
time: 35.4 us; the launch traced here: 35.3 us
  Pallas kernels  32.4 us (92%)
  local copies, waits for them, and re-layouts  1.55 us (4%)
  between operations  1.29 us (4%)
    pallas_call x1, Pallas kernels, body(): pl.pallas_call(functools.partial(kernel, sizes), out_shape=(pltpu.VMEM((h...  32.4 us
    unnamed x2, local copies, waits for them, and re-layouts  1.55 us

profile of v5, /device:TPU:0, one launch (start us, length us, event | category | flops | bytes accessed | tf_op | source)
XLA Modules:
  0.0 35.3 jit_solution(14614115552307432833)
XLA Ops:
  1.3 32.4 %shard_map.77 = (f32[4,256,256]{2,1,0:T(8,128)S(1)}, f32[1,512]{1,0:T(1,128)S(1)}) custom-call(f32[256,256]{1,0:T(8,128)} %kappa_hbm.1, f32[256,256]{1,0:T(8,128)} %tau_hbm.1, f32[1,512]{1,0:T(1,128)} %bitcast.4, f32[1,512]{1,0:T(1,128)} %bitcast.5, s32[3,512]{1,0:T(4,128)} %cell_hbm.1, s32[1]{0:T(128)S(6)} %copy.12.blocks_ref), custom_call_target="tpu_custom_call" | custom-call | tf_op jit(solution)/shard_map/pallas_call | solution.py:672
  33.7 1.0 %copy.10 = f32[4,256,256]{2,1,0:T(8,128)} copy(f32[4,256,256]{2,1,0:T(8,128)S(1)} %get-tuple-element.6) | data formatting | bytes 2097152
  34.7 0.6 %copy.11 = f32[512]{0:T(512)} copy(f32[512]{0:T(512)S(1)} %bitcast.3) | data formatting | bytes 4096
